TPU v7x, 32 devices: a whole 2x2x4 slice. The times are simulated.
32 devices in a mesh: dp: 4 (over z), ctx: 4 (over x, core), tp: 2 (over y).
Axes of the slice: x: 2, y: 2, z: 4, core: 2. Of those that a mesh axis runs over, the one named last changes fastest.
Arguments:
- latents_in: bfloat16 [12, 1024, 768], P('dp', 'ctx'), may hold values from -6 to 6
- condition: float32 [12, 768], P('dp'), may hold values from -6 to 6
- out_grad: bfloat16 [12, 1024, 768], P('dp', 'ctx'), may hold values from -6 to 6
- mod_weight: bfloat16 [2, 768, 4608], P(None, 'dp', 'tp'), may hold values from -0.21875 to 0.21875
- mod_bias: bfloat16 [2, 6, 768], P(None, 'tp', 'dp'), may hold values from -3 to 3
- qkv_weight: bfloat16 [2, 3, 768, 768], P(None, None, 'dp', 'tp'), may hold values from -0.21875 to 0.21875
- qkv_bias: bfloat16 [2, 2, 12, 64], P(None, None, 'tp', 'dp'), may hold values from -3 to 3
- proj_weight: bfloat16 [2, 768, 768], P(None, 'dp', 'tp'), may hold values from -2.5 to 2.5
- proj_bias: bfloat16 [2, 768], P(None, 'dp'), may hold values from -3 to 3
- fc1_weight: bfloat16 [2, 768, 3072], P(None, 'dp', 'tp'), may hold values from -0.21875 to 0.21875
- fc1_bias: bfloat16 [2, 24, 128], P(None, 'tp', 'dp'), may hold values from -3 to 3
- fc2_weight: bfloat16 [2, 768, 3072], P(None, 'dp', 'tp'), may hold values from -0.109375 to 0.109375
- fc2_bias: bfloat16 [2, 768], P(None, 'dp'), may hold values from -3 to 3
Outputs:
- block_out: bfloat16 [12, 1024, 768], P('dp', 'ctx')
- latents_grad: float32 [12, 1024, 768], P('dp', 'ctx')
- condition_grad: float32 [12, 768], P('dp')
- mod_weight_grad: float32 [2, 768, 4608], P(None, 'dp', 'tp')
- mod_bias_grad: float32 [2, 6, 768], P(None, 'tp', 'dp')
- qkv_weight_grad: float32 [2, 3, 768, 768], P(None, None, 'dp', 'tp')
- qkv_bias_grad: float32 [2, 2, 12, 64], P(None, None, 'tp', 'dp')
- proj_weight_grad: float32 [2, 768, 768], P(None, 'dp', 'tp')
- proj_bias_grad: float32 [2, 768], P(None, 'dp')
- fc1_weight_grad: float32 [2, 768, 3072], P(None, 'dp', 'tp')
- fc1_bias_grad: float32 [2, 24, 128], P(None, 'tp', 'dp')
- fc2_weight_grad: float32 [2, 768, 3072], P(None, 'dp', 'tp')
- fc2_bias_grad: float32 [2, 768], P(None, 'dp')
All inputs are finite; a program needn't handle non-finite values.
Results may differ from a plain program's by a relative error of at most 0.02.
The roundings to bfloat16 on the way count: a program that leaves them out, or rounds other values in their place, can miss the bound.
Values may be sent and summed in bfloat16 or wider, within the bound.
No kernel may reach another device: no remote copies, remote signals or barrier semaphores. Data moves between devices by JAX's collectives and lax.ppermute only.
A program may use at most 256 MiB of HBM per device.

v0:
```python
import jax
import jax.numpy as jnp
from jax import lax
from jax.sharding import PartitionSpec as P

PRECISE = lax.Precision.HIGHEST
EPSILON = 1e-06


def normalize(field):
    centre = field - jnp.mean(field, axis=-1, keepdims=True)
    scaling = lax.rsqrt(jnp.mean(centre * centre, axis=-1, keepdims=True) + EPSILON)
    return (centre * scaling, scaling)


def norm_back(upstream, normed, scaling):
    first = jnp.mean(upstream, axis=-1, keepdims=True)
    second = jnp.mean(upstream * normed, axis=-1, keepdims=True)
    return scaling * (upstream - first - normed * second)


def activation(field):
    return jax.nn.gelu(field, approximate=True)


def layer_slices(arrays, layer_no):
    return tuple((member[layer_no] for member in arrays))


def fetch_weights(shards):
    (
        mod_weight,
        mod_bias,
        qkv_weight,
        qkv_bias,
        proj_weight,
        proj_bias,
        fc1_weight,
        fc1_bias,
        fc2_weight,
        fc2_bias,
    ) = shards
    return (
        lax.all_gather(mod_weight, "dp", axis=0, tiled=True),
        lax.all_gather(mod_bias, "dp", axis=1, tiled=True),
        lax.all_gather(qkv_weight, "dp", axis=1, tiled=True),
        lax.all_gather(qkv_bias, "dp", axis=2, tiled=True),
        lax.all_gather(proj_weight, "dp", axis=0, tiled=True),
        lax.all_gather(proj_bias, "dp", axis=0, tiled=True),
        lax.all_gather(fc1_weight, "dp", axis=0, tiled=True),
        lax.all_gather(fc1_bias, "dp", axis=1, tiled=True),
        lax.all_gather(fc2_weight, "dp", axis=0, tiled=True),
        lax.all_gather(fc2_bias, "dp", axis=0, tiled=True),
    )


def reduce_grads(grads):
    (
        mod_wgrad,
        mod_bgrad,
        qkv_wgrad,
        qkv_bgrad,
        proj_wgrad,
        proj_bgrad,
        up_wgrad,
        up_bgrad,
        down_wgrad,
        down_bgrad,
    ) = grads
    shards = (
        lax.psum_scatter(mod_wgrad, "dp", scatter_dimension=0, tiled=True),
        lax.psum_scatter(mod_bgrad, "dp", scatter_dimension=1, tiled=True),
        lax.psum_scatter(qkv_wgrad, "dp", scatter_dimension=1, tiled=True),
        lax.psum_scatter(qkv_bgrad, "dp", scatter_dimension=2, tiled=True),
        lax.psum_scatter(proj_wgrad, "dp", scatter_dimension=0, tiled=True),
        lax.psum_scatter(proj_bgrad, "dp", scatter_dimension=0, tiled=True),
        lax.psum_scatter(up_wgrad, "dp", scatter_dimension=0, tiled=True),
        lax.psum_scatter(up_bgrad, "dp", scatter_dimension=1, tiled=True),
        lax.psum_scatter(down_wgrad, "dp", scatter_dimension=0, tiled=True),
        lax.psum_scatter(down_bgrad, "dp", scatter_dimension=0, tiled=True),
    )
    (
        mod_wpart,
        mod_bpart,
        qkv_wpart,
        qkv_bpart,
        proj_wpart,
        proj_bpart,
        up_wpart,
        up_bpart,
        down_wpart,
        down_bpart,
    ) = shards
    return lax.psum(
        (
            mod_wpart,
            mod_bpart,
            qkv_wpart,
            qkv_bpart,
            proj_wpart,
            proj_bpart,
            up_wpart,
            up_bpart,
            down_wpart,
            down_bpart,
        ),
        "ctx",
    )


def branch_reduce(part):
    return lax.psum(part, "tp")


def block_forward(resid, silu_cond, weights):
    (
        mod_weight,
        mod_bias,
        qkv_weight,
        qkv_bias,
        proj_weight,
        proj_bias,
        fc1_weight,
        fc1_bias,
        fc2_weight,
        fc2_bias,
    ) = weights
    latents = resid.shape[0]
    width = resid.shape[2]
    halfmod = jnp.dot(
        silu_cond, mod_weight.astype(jnp.float32), precision=PRECISE
    ) + mod_bias.astype(jnp.float32).reshape(-1)
    halfmod = halfmod.reshape(latents, mod_bias.shape[0], width)
    modulation = lax.all_gather(halfmod, "tp", axis=1, tiled=True)
    shift_one = modulation[:, 0:1, :]
    scale_one = modulation[:, 1:2, :]
    gate_one = modulation[:, 2:3, :]
    shift_two = modulation[:, 3:4, :]
    scale_two = modulation[:, 4:5, :]
    gate_two = modulation[:, 5:6, :]
    normed_one, scaling_one = normalize(resid)
    entry_one = (normed_one * (1.0 + scale_one) + shift_one).astype(jnp.bfloat16)
    tokens = entry_one.shape[1]
    projected = jnp.einsum(
        "bsd,tde->tbse", entry_one, qkv_weight, preferred_element_type=jnp.float32
    )
    bias_flat = qkv_bias.astype(jnp.float32).reshape(2, -1)
    queries = (projected[0] + bias_flat[0]).astype(jnp.bfloat16)
    keys_own = projected[1].astype(jnp.bfloat16)
    values_own = (projected[2] + bias_flat[1]).astype(jnp.bfloat16)
    keys_all, values_all = (
        lax.all_gather(keys_own, "ctx", axis=1, tiled=True),
        lax.all_gather(values_own, "ctx", axis=1, tiled=True),
    )
    heads = qkv_bias.shape[1]
    head_size = qkv_bias.shape[2]
    factor = head_size ** (-0.5)
    query_heads = queries.reshape(latents, tokens, heads, head_size)
    key_heads = keys_all.reshape(latents, -1, heads, head_size)
    value_heads = values_all.reshape(latents, -1, heads, head_size)
    scores = (
        jnp.einsum("bqhd,bkhd->bhqk", query_heads, key_heads, preferred_element_type=jnp.float32)
        * factor
    )
    highest = jnp.max(scores, axis=-1, keepdims=True)
    logsum = highest + jnp.log(jnp.sum(jnp.exp(scores - highest), axis=-1, keepdims=True))
    probs_low = jnp.exp(scores - logsum).astype(jnp.bfloat16)
    context = jnp.einsum(
        "bhqk,bkhd->bqhd", probs_low, value_heads, preferred_element_type=jnp.float32
    )
    context = context.reshape(latents, tokens, -1).astype(jnp.bfloat16)
    attn_part = jnp.einsum("bsi,oi->bso", context, proj_weight, preferred_element_type=jnp.float32)
    attended = branch_reduce(attn_part) + proj_bias.astype(jnp.float32)
    middle = resid + gate_one * attended
    normed_two, scaling_two = normalize(middle)
    entry_two = (normed_two * (1.0 + scale_two) + shift_two).astype(jnp.bfloat16)
    hidden_pre = jnp.einsum(
        "bsd,df->bsf", entry_two, fc1_weight, preferred_element_type=jnp.float32
    ) + fc1_bias.astype(jnp.float32).reshape(-1)
    hidden = activation(hidden_pre).astype(jnp.bfloat16)
    mlp_part = jnp.einsum("bsf,of->bso", hidden, fc2_weight, preferred_element_type=jnp.float32)
    mlp_out = branch_reduce(mlp_part) + fc2_bias.astype(jnp.float32)
    result = middle + gate_two * mlp_out
    saved = (
        modulation,
        normed_one,
        scaling_one,
        entry_one,
        queries,
        keys_all,
        values_all,
        logsum,
        context,
        attended,
        normed_two,
        scaling_two,
        entry_two,
        hidden_pre,
        hidden,
        mlp_out,
    )
    return (result, saved)


def block_backward(upstream, silu_cond, weights, saved):
    (
        mod_weight,
        mod_bias,
        qkv_weight,
        qkv_bias,
        proj_weight,
        proj_bias,
        fc1_weight,
        fc1_bias,
        fc2_weight,
        fc2_bias,
    ) = weights
    (
        modulation,
        normed_one,
        scaling_one,
        entry_one,
        queries,
        keys_all,
        values_all,
        logsum,
        context,
        attended,
        normed_two,
        scaling_two,
        entry_two,
        hidden_pre,
        hidden,
        mlp_out,
    ) = saved
    latents = upstream.shape[0]
    tokens = entry_one.shape[1]
    scale_one = modulation[:, 1:2, :]
    gate_one = modulation[:, 2:3, :]
    scale_two = modulation[:, 4:5, :]
    gate_two = modulation[:, 5:6, :]
    gate_two_grad = jnp.sum(upstream * mlp_out, axis=1)
    mlp_grad = (gate_two * upstream).astype(jnp.bfloat16)
    fc2_grad = jnp.einsum("bso,bsf->of", mlp_grad, hidden, preferred_element_type=jnp.float32)
    fc2_bias_grad = jnp.sum(mlp_grad, axis=(0, 1), dtype=jnp.float32)
    hidden_grad = jnp.einsum(
        "bso,of->bsf", mlp_grad, fc2_weight, preferred_element_type=jnp.float32
    )
    unused_value, gelu_pull = jax.vjp(activation, hidden_pre)
    pre_grad = gelu_pull(hidden_grad)[0].astype(jnp.bfloat16)
    fc1_grad = jnp.einsum("bsd,bsf->df", entry_two, pre_grad, preferred_element_type=jnp.float32)
    fc1_bias_grad = jnp.sum(pre_grad, axis=(0, 1), dtype=jnp.float32).reshape(fc1_bias.shape)
    entry_two_part = jnp.einsum(
        "bsf,df->bsd", pre_grad, fc1_weight, preferred_element_type=jnp.float32
    )
    entry_two_grad = branch_reduce(entry_two_part)
    scale_two_grad = jnp.sum(entry_two_grad * normed_two, axis=1)
    shift_two_grad = jnp.sum(entry_two_grad, axis=1)
    middle_grad = upstream + norm_back(entry_two_grad * (1.0 + scale_two), normed_two, scaling_two)
    gate_one_grad = jnp.sum(middle_grad * attended, axis=1)
    attended_grad = (gate_one * middle_grad).astype(jnp.bfloat16)
    proj_grad = jnp.einsum(
        "bso,bsi->oi", attended_grad, context, preferred_element_type=jnp.float32
    )
    proj_bias_grad = jnp.sum(attended_grad, axis=(0, 1), dtype=jnp.float32)
    context_grad = jnp.einsum(
        "bso,oi->bsi", attended_grad, proj_weight, preferred_element_type=jnp.float32
    ).astype(jnp.bfloat16)
    heads = qkv_bias.shape[1]
    head_size = qkv_bias.shape[2]
    factor = head_size ** (-0.5)
    query_heads = queries.reshape(latents, tokens, heads, head_size)
    key_heads = keys_all.reshape(latents, -1, heads, head_size)
    value_heads = values_all.reshape(latents, -1, heads, head_size)
    context_heads = context_grad.reshape(latents, tokens, heads, head_size)
    scores = (
        jnp.einsum("bqhd,bkhd->bhqk", query_heads, key_heads, preferred_element_type=jnp.float32)
        * factor
    )
    probs = jnp.exp(scores - logsum)
    probs_low = probs.astype(jnp.bfloat16)
    prob_grad = jnp.einsum(
        "bqhd,bkhd->bhqk", context_heads, value_heads, preferred_element_type=jnp.float32
    )
    row_terms = jnp.sum(probs * prob_grad, axis=-1, keepdims=True)
    score_grad = (probs * (prob_grad - row_terms) * factor).astype(jnp.bfloat16)
    query_grad = jnp.einsum(
        "bhqk,bkhd->bqhd", score_grad, key_heads, preferred_element_type=jnp.float32
    )
    query_grad = query_grad.reshape(latents, tokens, -1).astype(jnp.bfloat16)
    key_part = jnp.einsum(
        "bhqk,bqhd->bkhd", score_grad, query_heads, preferred_element_type=jnp.float32
    ).reshape(latents, keys_all.shape[1], -1)
    value_part = jnp.einsum(
        "bhqk,bqhd->bkhd", probs_low, context_heads, preferred_element_type=jnp.float32
    ).reshape(latents, keys_all.shape[1], -1)
    key_grad, value_grad = (
        lax.psum_scatter(key_part, "ctx", scatter_dimension=1, tiled=True),
        lax.psum_scatter(value_part, "ctx", scatter_dimension=1, tiled=True),
    )
    stacked = jnp.stack(
        [query_grad, key_grad.astype(jnp.bfloat16), value_grad.astype(jnp.bfloat16)]
    )
    qkv_grad = jnp.einsum("bsd,tbse->tde", entry_one, stacked, preferred_element_type=jnp.float32)
    qkv_bias_grad = jnp.stack(
        [
            jnp.sum(stacked[0], axis=(0, 1), dtype=jnp.float32),
            jnp.sum(stacked[2], axis=(0, 1), dtype=jnp.float32),
        ]
    ).reshape(qkv_bias.shape)
    entry_one_part = jnp.einsum(
        "tbse,tde->bsd", stacked, qkv_weight, preferred_element_type=jnp.float32
    )
    entry_one_grad = branch_reduce(entry_one_part)
    scale_one_grad = jnp.sum(entry_one_grad * normed_one, axis=1)
    shift_one_grad = jnp.sum(entry_one_grad, axis=1)
    resid_grad = middle_grad + norm_back(
        entry_one_grad * (1.0 + scale_one), normed_one, scaling_one
    )
    mod_grad = jnp.stack(
        [
            shift_one_grad,
            scale_one_grad,
            gate_one_grad,
            shift_two_grad,
            scale_two_grad,
            gate_two_grad,
        ],
        axis=1,
    )
    share = mod_bias.shape[0]
    own_grad = lax.dynamic_slice_in_dim(mod_grad, lax.axis_index("tp") * share, share, 1)
    own_flat = own_grad.reshape(latents, -1)
    mod_wgrad = jnp.dot(silu_cond.T, own_flat, precision=PRECISE)
    mod_bgrad = jnp.sum(own_grad, axis=0)
    cond_part = jnp.dot(own_flat, mod_weight.astype(jnp.float32).T, precision=PRECISE)
    grads = (
        mod_wgrad,
        mod_bgrad,
        qkv_grad,
        qkv_bias_grad,
        proj_grad,
        proj_bias_grad,
        fc1_grad,
        fc1_bias_grad,
        fc2_grad,
        fc2_bias_grad,
    )
    return (resid_grad, grads, cond_part)


def local(
    latents_in,
    condition,
    out_grad,
    mod_weight,
    mod_bias,
    qkv_weight,
    qkv_bias,
    proj_weight,
    proj_bias,
    fc1_weight,
    fc1_bias,
    fc2_weight,
    fc2_bias,
):
    arrays = (
        mod_weight,
        mod_bias,
        qkv_weight,
        qkv_bias,
        proj_weight,
        proj_bias,
        fc1_weight,
        fc1_bias,
        fc2_weight,
        fc2_bias,
    )
    layers = mod_weight.shape[0]
    resid = latents_in.astype(jnp.float32)
    upstream = out_grad.astype(jnp.float32)
    silu_cond = jax.nn.silu(condition)
    kept_weights = []
    saved_list = []
    for layer_no in range(layers):
        weights = fetch_weights(layer_slices(arrays, layer_no))
        resid, saved = block_forward(resid, silu_cond, weights)
        kept_weights.append(weights)
        saved_list.append(saved)
    cond_total = jnp.zeros(condition.shape, jnp.float32)
    results = [None] * layers
    for layer_no in reversed(range(layers)):
        weights = kept_weights[layer_no]
        upstream, grads, cond_part = block_backward(
            upstream, silu_cond, weights, saved_list[layer_no]
        )
        results[layer_no] = reduce_grads(grads)
        cond_total = cond_total + cond_part
    block_out = resid.astype(jnp.bfloat16)
    cond_sum = lax.psum(cond_total, ("ctx", "tp"))
    unused_value, silu_pull = jax.vjp(jax.nn.silu, condition)
    condition_grad = silu_pull(cond_sum)[0]
    stacked = [
        jnp.stack([results[layer_no][member] for layer_no in range(layers)]) for member in range(10)
    ]
    return (
        block_out,
        upstream,
        condition_grad,
        stacked[0],
        stacked[1],
        stacked[2],
        stacked[3],
        stacked[4],
        stacked[5],
        stacked[6],
        stacked[7],
        stacked[8],
        stacked[9],
    )


def solution(mesh):
    placed = (
        P("dp", "ctx", None),
        P("dp", None),
        P("dp", "ctx", None),
        P(None, "dp", "tp"),
        P(None, "tp", "dp"),
        P(None, None, "dp", "tp"),
        P(None, None, "tp", "dp"),
        P(None, "dp", "tp"),
        P(None, "dp"),
        P(None, "dp", "tp"),
        P(None, "tp", "dp"),
        P(None, "dp", "tp"),
        P(None, "dp"),
    )
    return jax.shard_map(
        local,
        mesh=mesh,
        in_specs=placed,
        out_specs=(
            P("dp", "ctx", None),
            P("dp", "ctx", None),
            P("dp", None),
            P(None, "dp", "tp"),
            P(None, "tp", "dp"),
            P(None, None, "dp", "tp"),
            P(None, None, "tp", "dp"),
            P(None, "dp", "tp"),
            P(None, "dp"),
            P(None, "dp", "tp"),
            P(None, "tp", "dp"),
            P(None, "dp", "tp"),
            P(None, "dp"),
        ),
        check_vma=False,
    )
```

profile of v0, /device:TPU:0, one launch (start us, length us, event | category | flops | bytes accessed | tf_op | source)
XLA Modules:
  0.0 2612.2 jit_solution(15465557252555220215)
XLA Ops:
  32.2 52.7 %all-gather.39.cloned.1.call-done = bf16[1,768,2304]{2,1,0:T(8,128)(2,1)} async-done(((bf16[1,192,2304]{2,1,0:T(8,128)(2,1)}), bf16[1,768,2304]{2,1,0:T(8,128)(2,1)}) %all-gather.39.cloned.1.call-update) | async-done | bytes 3538960 | tf_op jit(solution)/shard_map/all_gather | solution.py:44
  277.5 50.0 %all-gather.45.cloned.1.call-done = bf16[1,768,1536]{2,1,0:T(8,128)(2,1)} async-done(((bf16[1,192,1536]{2,1,0:T(8,128)(2,1)}), bf16[1,768,1536]{2,1,0:T(8,128)(2,1)}) %all-gather.45.cloned.1.call-update) | async-done | bytes 2359312 | tf_op jit(solution)/shard_map/all_gather | solution.py:50
  333.4 45.6 %all-gather.47.cloned.1.call-done = bf16[1,768,1536]{2,1,0:T(8,128)(2,1)} async-done(((bf16[1,192,1536]{2,1,0:T(8,128)(2,1)}), bf16[1,768,1536]{2,1,0:T(8,128)(2,1)}) %all-gather.47.cloned.1.call-update) | async-done | bytes 2359312 | tf_op jit(solution)/shard_map/all_gather | solution.py:52
  405.5 49.8 %all-gather.49.cloned.1.call-done = bf16[1,768,2304]{2,1,0:T(8,128)(2,1)} async-done(((bf16[1,192,2304]{2,1,0:T(8,128)(2,1)}), bf16[1,768,2304]{2,1,0:T(8,128)(2,1)}) %all-gather.49.cloned.1.call-update) | async-done | bytes 3538960 | tf_op jit(solution)/shard_map/all_gather | solution.py:44
  464.0 62.1 %all-reduce.24.cloned.1.call-done = f32[3,256,768]{2,1,0:T(8,128)} async-done(((f32[3,256,768]{2,1,0:T(8,128)}), f32[3,256,768]{2,1,0:T(8,128)}) %all-reduce.24.cloned.1.call-update) | async-done | bytes 2359312 | tf_op jit(solution)/shard_map/psum | solution.py:112
  529.4 38.5 %all-gather.51.cloned.1.call-done = bf16[1,3,768,384]{3,2,1,0:T(8,128)(2,1)} async-done(((bf16[1,3,192,384]{3,2,1,0:T(8,128)(2,1)}), bf16[1,3,768,384]{3,2,1,0:T(8,128)(2,1)}) %all-gather.51.cloned.1.call-update) | async-done | bytes 1769488 | tf_op jit(solution)/shard_map/all_gather | solution.py:46
  659.2 53.1 %all-reduce.26.cloned.1.call-done = f32[3,256,768]{2,1,0:T(8,128)} async-done(((f32[3,256,768]{2,1,0:T(8,128)}), f32[3,256,768]{2,1,0:T(8,128)}) %all-reduce.26.cloned.1.call-update) | async-done | bytes 2359312 | tf_op jit(solution)/shard_map/psum | solution.py:112
  716.5 47.9 %all-gather.55.cloned.1.call-done = bf16[1,768,1536]{2,1,0:T(8,128)(2,1)} async-done(((bf16[1,192,1536]{2,1,0:T(8,128)(2,1)}), bf16[1,768,1536]{2,1,0:T(8,128)(2,1)}) %all-gather.55.cloned.1.call-update) | async-done | bytes 2359312 | tf_op jit(solution)/shard_map/all_gather | solution.py:50
  770.4 45.4 %all-gather.57.cloned.1.call-done = bf16[1,768,1536]{2,1,0:T(8,128)(2,1)} async-done(((bf16[1,192,1536]{2,1,0:T(8,128)(2,1)}), bf16[1,768,1536]{2,1,0:T(8,128)(2,1)}) %all-gather.57.cloned.1.call-update) | async-done | bytes 2359312 | tf_op jit(solution)/shard_map/all_gather | solution.py:52
  828.5 67.5 %all-reduce.28.cloned.1.call-done = f32[3,256,768]{2,1,0:T(8,128)} async-done(((f32[3,256,768]{2,1,0:T(8,128)}), f32[3,256,768]{2,1,0:T(8,128)}) %all-reduce.28.cloned.1.call-update) | async-done | bytes 2359312 | tf_op jit(solution)/shard_map/psum | solution.py:112
  932.5 37.4 %fusion.11 = f32[3,6,64,1024]{3,2,1,0:T(8,128)} fusion(f32[3,6,256,1024]{3,2,1,0:T(8,128)} %fusion.202, f32[3,6,256,1024]{3,2,1,0:T(8,128)} %get-tuple-element.191, f32[3,6,256]{2,1,0:T(8,128)S(1)} %copy-done.64, f32[3,256,6,64]{1,3,2,0:T(8,128)} %bitcast.331, f32[6,64]{1,0:T(8,128)S(1)} %copy-done.83), kind=kOutput, calls=%fused_computation.16 | convolution fusion | flops 647042560 | bytes 43666944 | tf_op jit(solution)/shard_map/bhqk,bqhd->bkhd/dot_general | solution.py:291
  1030.4 68.5 %all-reduce.30.cloned.1.call-done = f32[3,256,768]{2,1,0:T(8,128)} async-done(((f32[3,256,768]{2,1,0:T(8,128)}), f32[3,256,768]{2,1,0:T(8,128)}) %all-reduce.30.cloned.1.call-update) | async-done | bytes 2359312 | tf_op jit(solution)/shard_map/psum | solution.py:112
  1117.3 68.7 %all-reduce.32.cloned.1.call-done = f32[3,256,768]{2,1,0:T(8,128)} async-done(((f32[3,256,768]{2,1,0:T(8,128)}), f32[3,256,768]{2,1,0:T(8,128)}) %all-reduce.32.cloned.1.call-update) | async-done | bytes 2359312 | tf_op jit(solution)/shard_map/psum | solution.py:112
  1227.3 44.3 %fusion.17 = f32[3,6,64,1024]{3,2,1,0:T(8,128)} fusion(f32[3,6,256,1024]{3,2,1,0:T(8,128)} %fusion.203, f32[3,6,256,1024]{3,2,1,0:T(8,128)} %get-tuple-element.189, f32[3,6,256]{2,1,0:T(8,128)} %log_add_fusion.1, f32[3,256,6,64]{1,3,2,0:T(8,128)} %bitcast.329, f32[6,64]{1,0:T(8,128)S(1)} %copy-done.81), kind=kOutput, calls=%fused_computation.18 | convolution fusion | flops 647042560 | bytes 43666944 | tf_op jit(solution)/shard_map/bhqk,bqhd->bkhd/dot_general | solution.py:291
  1285.9 43.2 %convert_reduce_fusion.10 = (f32[6,64]{1,0:T(8,128)}, bf16[3,6,64,256]{3,2,1,0:T(8,128)(2,1)S(1)}) fusion(bf16[3,1024,6,64]{1,3,2,0:T(8,128)(2,1)} %bitcast.317, f32[3,6,256,1024]{3,2,1,0:T(8,128)} %fusion.203, f32[3,6,256,1024]{3,2,1,0:T(8,128)} %get-tuple-element.189, f32[3,6,256]{2,1,0:T(8,128)} %log_add_fusion.1), kind=kOutput, calls=%fused_computation.177 | convolution fusion | flops 647337088 | bytes 40717824 | tf_op jit(solution)/shard_map/bhqk,bkhd->bqhd/dot_general | solution.py:287
  1417.1 42.0 %all-reduce.36.cloned.1.call-done = (f32[3,256,768]{2,1,0:T(8,128)}, f32[3,256,768]{2,1,0:T(8,128)}) async-done(((f32[3,256,768]{2,1,0:T(8,128)}, f32[3,256,768]{2,1,0:T(8,128)}), (f32[3,256,768]{2,1,0:T(8,128)}, f32[3,256,768]{2,1,0:T(8,128)})) %all-reduce.36.cloned.1.call-update) | async-done | bytes 4718608 | tf_op jit(solution)/shard_map/psum | solution.py:112
  1531.3 66.2 %reduce-scatter.65.cloned.1.call-done = f32[192,1152]{1,0:T(8,128)} async-done(((f32[768,1152]{1,0:T(8,128)}), f32[192,1152]{1,0:T(8,128)}) %reduce-scatter.65.cloned.1.call-update) | async-done | bytes 884752
  1629.3 86.2 %reduce-scatter.59.cloned.1.call-done = f32[192,1536]{1,0:T(8,128)} async-done(((f32[768,1536]{1,0:T(8,128)}), f32[192,1536]{1,0:T(8,128)}) %reduce-scatter.59.cloned.1.call-update) | async-done | bytes 1179664 | tf_op jit(solution)/shard_map/reduce_scatter | solution.py:79
  1715.5 88.2 %reduce-scatter.55.cloned.1.call-done = f32[192,1536]{1,0:T(8,128)} async-done(((f32[768,1536]{1,0:T(8,128)}), f32[192,1536]{1,0:T(8,128)}) %reduce-scatter.55.cloned.1.call-update) | async-done | bytes 1179664 | tf_op jit(solution)/shard_map/reduce_scatter | solution.py:77
  1835.9 86.2 %reduce-scatter.57.cloned.1.call-done = f32[192,1536]{1,0:T(8,128)} async-done(((f32[768,1536]{1,0:T(8,128)}), f32[192,1536]{1,0:T(8,128)}) %reduce-scatter.57.cloned.1.call-update) | async-done | bytes 1179664 | tf_op jit(solution)/shard_map/reduce_scatter | solution.py:79
  1922.1 88.2 %reduce-scatter.53.cloned.1.call-done = f32[192,1536]{1,0:T(8,128)} async-done(((f32[768,1536]{1,0:T(8,128)}), f32[192,1536]{1,0:T(8,128)}) %reduce-scatter.53.cloned.1.call-update) | async-done | bytes 1179664 | tf_op jit(solution)/shard_map/reduce_scatter | solution.py:77
  2010.4 126.5 %reduce-scatter.45.cloned.1.call-done = f32[192,2304]{1,0:T(8,128)} async-done(((f32[768,2304]{1,0:T(8,128)}), f32[192,2304]{1,0:T(8,128)}) %reduce-scatter.45.cloned.1.call-update) | async-done | bytes 1769488 | tf_op jit(solution)/shard_map/reduce_scatter | solution.py:71
  2136.8 126.3 %reduce-scatter.47.cloned.1.call-done = f32[192,2304]{1,0:T(8,128)} async-done(((f32[768,2304]{1,0:T(8,128)}), f32[192,2304]{1,0:T(8,128)}) %reduce-scatter.47.cloned.1.call-update) | async-done | bytes 1769488 | tf_op jit(solution)/shard_map/reduce_scatter | solution.py:71
  2417.9 174.5 %all-reduce.34.cloned.1.call-done = (f32[1,192,2304]{2,1,0:T(8,128)}, f32[1,192,2304]{2,1,0:T(8,128)}, f32[1,3,192,384]{2,3,1,0:T(8,128)}, f32[1,3,192,384]{2,3,...) async-done(((f32[1,192,2304]{2,1,0:T(8,128)}, ...) | async-done | bytes 10616848 | tf_op jit(solution)/shard_map/psum | solution.py:94
  (634 shorter events, 935.0 us)
Async XLA Ops:
  209.2 246.1 %all-gather.49.cloned.1.call-start = ((), (), s32[]{:S(2)}) async-start(), calls=%async_computation.45 | async-start | bytes 4423680 | tf_op jit(solution)/shard_map/all_gather | solution.py:44
  209.9 316.2 %all-reduce.24.cloned.1.call-start = ((), (), s32[]{:S(2)}) async-start(), calls=%async_computation.22 | async-start | bytes 4718592 | tf_op jit(solution)/shard_map/psum | solution.py:112
  387.2 219.7 %all-gather.53.cloned.1.call-start = ((), (), s32[]{:S(2)}) async-start(), calls=%async_computation.47 | async-start | bytes 2949120 | tf_op jit(solution)/shard_map/all_gather | solution.py:152
  645.0 251.0 %all-reduce.28.cloned.1.call-start = ((), (), s32[]{:S(2)}) async-start(), calls=%async_computation.25 | async-start | bytes 4718592 | tf_op jit(solution)/shard_map/psum | solution.py:112
  828.5 186.3 %reduce-scatter.39.cloned.1.call-start = ((), (), s32[]{:S(2)}) async-start(), calls=%async_computation.27 | async-start | bytes 5898240 | tf_op jit(solution)/shard_map/reduce_scatter | solution.py:299
  1117.2 212.9 %reduce-scatter.43.cloned.1.call-start = ((), (), s32[]{:S(2)}) async-start(), calls=%async_computation.31 | async-start | bytes 5898240 | tf_op jit(solution)/shard_map/reduce_scatter | solution.py:299
  1277.7 181.4 %all-reduce.36.cloned.1.call-start = ((), (), s32[]{:S(2)}) async-start(), calls=%async_computation.59 | async-start | bytes 9437184 | tf_op jit(solution)/shard_map/psum | solution.py:112
  1339.5 188.9 %reduce-scatter.67.cloned.1.call-start = ((), (), s32[]{:S(2)}) async-start(), calls=%async_computation.53 | async-start | bytes 4423680
  1356.0 241.5 %reduce-scatter.65.cloned.1.call-start = ((), (), s32[]{:S(2)}) async-start(), calls=%async_computation.52 | async-start | bytes 4423680
  1372.1 257.1 %reduce-scatter.51.cloned.1.call-start = ((), (), s32[]{:S(2)}) async-start(), calls=%async_computation.35 | async-start | bytes 1474560 | tf_op jit(solution)/shard_map/reduce_scatter | solution.py:75
  1376.4 339.1 %reduce-scatter.59.cloned.1.call-start = ((), (), s32[]{:S(2)}) async-start(), calls=%async_computation.39 | async-start | bytes 5898240 | tf_op jit(solution)/shard_map/reduce_scatter | solution.py:79
  1383.4 420.4 %reduce-scatter.55.cloned.1.call-start = ((), (), s32[]{:S(2)}) async-start(), calls=%async_computation.37 | async-start | bytes 5898240 | tf_op jit(solution)/shard_map/reduce_scatter | solution.py:77
  1391.2 444.7 %reduce-scatter.49.cloned.1.call-start = ((), (), s32[]{:S(2)}) async-start(), calls=%async_computation.34 | async-start | bytes 1474560 | tf_op jit(solution)/shard_map/reduce_scatter | solution.py:75
  1394.6 527.5 %reduce-scatter.57.cloned.1.call-start = ((), (), s32[]{:S(2)}) async-start(), calls=%async_computation.38 | async-start | bytes 5898240 | tf_op jit(solution)/shard_map/reduce_scatter | solution.py:79
  1401.7 608.7 %reduce-scatter.53.cloned.1.call-start = ((), (), s32[]{:S(2)}) async-start(), calls=%async_computation.36 | async-start | bytes 5898240 | tf_op jit(solution)/shard_map/reduce_scatter | solution.py:77
  1409.3 727.6 %reduce-scatter.45.cloned.1.call-start = ((), (), s32[]{:S(2)}) async-start(), calls=%async_computation.32 | async-start | bytes 8847360 | tf_op jit(solution)/shard_map/reduce_scatter | solution.py:71
  1476.7 786.5 %reduce-scatter.47.cloned.1.call-start = ((), (), s32[]{:S(2)}) async-start(), calls=%async_computation.33 | async-start | bytes 8847360 | tf_op jit(solution)/shard_map/reduce_scatter | solution.py:71
  1484.6 800.4 %reduce-scatter.75.cloned.1.call-start = ((), (), s32[]{:S(2)}) async-start(), calls=%async_computation.57 | async-start | bytes 81920
  1486.0 818.4 %reduce-scatter.71.cloned.1.call-start = ((), (), s32[]{:S(2)}) async-start(), calls=%async_computation.55 | async-start | bytes 40960
  1487.2 836.6 %reduce-scatter.73.cloned.1.call-start = ((), (), s32[]{:S(2)}) async-start(), calls=%async_computation.56 | async-start | bytes 81920
  1488.0 855.0 %reduce-scatter.69.cloned.1.call-start = ((), (), s32[]{:S(2)}) async-start(), calls=%async_computation.54 | async-start | bytes 40960
  1489.1 910.9 %reduce-scatter.61.cloned.1.call-start = ((), (), s32[]{:S(2)}) async-start(), calls=%async_computation.50 | async-start | bytes 491520
  1490.1 910.8 %reduce-scatter.63.cloned.1.call-start = ((), (), s32[]{:S(2)}) async-start(), calls=%async_computation.51 | async-start | bytes 491520
  1491.4 1101.1 %all-reduce.34.cloned.1.call-start = ((), (), s32[]{:S(2)}) async-start(), calls=%async_computation.58 | async-start | bytes 22413312 | tf_op jit(solution)/shard_map/psum | solution.py:94
  (171 other events, 5539.1 us)
Sparse Core Ops, SparseCore 0:
  10.2 74.6 all-gather.38
  206.5 68.3 all-reduce.21
  277.0 50.4 all-gather.44
  329.7 49.2 all-gather.46
  381.3 73.9 all-gather.48
  458.3 67.8 all-reduce.23
  644.0 68.3 all-reduce.25
  713.9 50.4 all-gather.54
  766.4 49.2 all-gather.56
  828.6 67.4 all-reduce.27
  921.3 47.8 reduce-scatter.38
  976.2 47.8 reduce-scatter.36
  1030.3 68.6 all-reduce.29
  1117.3 68.6 all-reduce.31
  1339.6 119.4 all-reduce.35
  1462.0 66.3 reduce-scatter.66
  1530.8 66.6 reduce-scatter.64
  1631.5 83.9 reduce-scatter.58
  1717.9 85.7 reduce-scatter.54
  1838.2 83.9 reduce-scatter.56
  1924.6 85.7 reduce-scatter.52
  2012.8 124.0 reduce-scatter.44
  2139.1 124.0 reduce-scatter.46
  2391.6 200.7 all-reduce.33
  (16 shorter events, 436.0 us)
where the time goes:
time: 2620 us; the launch traced here: 2610 us
  waiting for transfers between devices  1790 us (68%)
  matrix products  383 us (15%)
  blocking collectives  198 us (8%)
  local copies, waits for them, and re-layouts  135 us (5%)
  other arithmetic  90.6 us (3%)
    psum x7, waiting for transfers between devices, branch_reduce(): return lax.psum(part, 'tp')  399 us
    reduce_scatter x2, waiting for transfers between devices, reduce_grads(): lax.psum_scatter(mod_wgrad, 'dp', scatter_dimension=0, tiled=True)  253 us
    unnamed x48, waiting for transfers between devices  179 us
    reduce_scatter x2, waiting for transfers between devices, reduce_grads(): lax.psum_scatter(up_wgrad, 'dp', scatter_dimension=0, tiled=True)  176 us
    psum x1, waiting for transfers between devices, reduce_grads(): lax.psum((mod_wpart, mod_bpart, qkv_wpart, qkv_bpart, proj_wpart, proj_bp...  175 us
    reduce_scatter x2, waiting for transfers between devices, reduce_grads(): lax.psum_scatter(down_wgrad, 'dp', scatter_dimension=0, tiled=True)  172 us
    all_gather x2, waiting for transfers between devices, fetch_weights(): lax.all_gather(mod_weight, 'dp', axis=0, tiled=True)  103 us
    all_gather x2, waiting for transfers between devices, fetch_weights(): lax.all_gather(fc1_weight, 'dp', axis=0, tiled=True)  97.9 us
  transfers between devices with their start and end apart: 40, of which 31 were waited for; matrix products, arithmetic and copies ran while one was open for 17% of the time, Pallas kernels for 0%

commit v1 on v0

v1 whole, which is shorter than its diff:
```python
import jax
import jax.numpy as jnp
from jax import lax
from jax.experimental import pallas as pl
from jax.experimental.pallas import tpu as pltpu
from jax.sharding import PartitionSpec as P

PRECISE = lax.Precision.HIGHEST
EPSILON = 1e-06
LOW = jnp.bfloat16
FULL = jnp.float32
CHIPS = ((0, 0), (0, 1), (1, 0), (1, 1))
PLANE = ("ctx", "tp")
VMEM_LIMIT = 56 * 1024 * 1024


def swap(value, x=0, core=0, y=0):
    mask = 4 * x + 2 * core + y
    return lax.ppermute(value, PLANE, [(at, at ^ mask) for at in range(8)])


def swap_dp(value, mask, count):
    return lax.ppermute(value, "dp", [(at, at ^ mask) for at in range(count)])


def pick(index, options):
    if len(options) == 1:
        return options[0]
    half = len(options) // 2
    low, high = pick(index % half, options[:half]), pick(index % half, options[half:])
    return jnp.where(index // half == 0, low, high)


def unrelate(pieces, index):
    return [pick(index, [pieces[place ^ at] for at in range(len(pieces))]) for place in range(len(pieces))]


class Place:
    def __init__(self, mesh):
        self.n_dp = mesh.shape["dp"]
        self.z = lax.axis_index("dp")
        self.ctx = lax.axis_index("ctx")
        self.x = self.ctx // 2
        self.core = self.ctx % 2
        self.y = lax.axis_index("tp")
        self.direct = self.n_dp <= 4 and self.n_dp & (self.n_dp - 1) == 0

    def gather_dp(self, value):
        if not self.direct:
            return lax.all_gather(value, "dp")
        pieces = [value] + [swap_dp(value, mask, self.n_dp) for mask in range(1, self.n_dp)]
        return jnp.stack(unrelate(pieces, self.z))

    def scatter_dp(self, value, dtype):
        if not self.direct:
            return lax.psum_scatter(value.astype(dtype), "dp", scatter_dimension=0).astype(FULL)
        total = lax.dynamic_index_in_dim(value, self.z, 0, keepdims=False)
        for mask in range(1, self.n_dp):
            part = lax.dynamic_index_in_dim(value, self.z ^ mask, 0, keepdims=False)
            total = total + swap_dp(part.astype(dtype), mask, self.n_dp).astype(FULL)
        return total

    def sum_plane(self, value):
        value = value + swap(value, core=1)
        value = value + swap(value, x=1)
        return value + swap(value, y=1)


def normalize(field):
    centre = field - jnp.mean(field, axis=-1, keepdims=True)
    scaling = lax.rsqrt(jnp.mean(centre * centre, axis=-1, keepdims=True) + EPSILON)
    return (centre * scaling, scaling)


def norm_back(upstream, normed, scaling):
    first = jnp.mean(upstream, axis=-1, keepdims=True)
    second = jnp.mean(upstream * normed, axis=-1, keepdims=True)
    return scaling * (upstream - first - normed * second)


def activation(field):
    return jax.nn.gelu(field, approximate=True)


def dot(left, right):
    return jnp.dot(left, right, preferred_element_type=FULL)


def dot_nt(left, right):
    return lax.dot_general(left, right, (((1,), (1,)), ((), ())), preferred_element_type=FULL)


def dot_tn(left, right):
    return lax.dot_general(left, right, (((0,), (0,)), ((), ())), preferred_element_type=FULL)


def attend_kernel(size, factor, own_ref, other_ref, out_ref, log_ref):
    chips, tokens, triple = own_ref.shape
    width = triple // 3
    own = own_ref[...].reshape(chips * tokens, triple)
    other = other_ref[...].reshape(chips * tokens, 2 * width)
    outs = []
    for head in range(width // size):
        lo, hi = head * size, (head + 1) * size
        queries = own[:, lo:hi] * jnp.asarray(factor, LOW)
        score_a = dot_nt(queries, own[:, width + lo : width + hi])
        score_b = dot_nt(queries, other[:, lo:hi])
        highest = jnp.maximum(
            jnp.max(score_a, axis=-1, keepdims=True), jnp.max(score_b, axis=-1, keepdims=True)
        )
        exp_a = jnp.exp(score_a - highest)
        exp_b = jnp.exp(score_b - highest)
        total = jnp.sum(exp_a, axis=-1, keepdims=True) + jnp.sum(exp_b, axis=-1, keepdims=True)
        inverse = 1.0 / total
        out = dot((exp_a * inverse).astype(LOW), own[:, 2 * width + lo : 2 * width + hi])
        out = out + dot((exp_b * inverse).astype(LOW), other[:, width + lo : width + hi])
        outs.append(out)
        log_ref[:, head : head + 1] = highest + jnp.log(total)
    out_ref[...] = jnp.concatenate(outs, axis=1).astype(LOW).reshape(chips, tokens, width)


def attend(own, other, size):
    chips, latents, tokens, triple = own.shape
    width = triple // 3
    heads = width // size
    rows = chips * tokens

    def block(columns):
        return pl.BlockSpec((chips, None, tokens, columns), lambda at: (0, at, 0, 0))

    return pl.pallas_call(
        lambda *refs: attend_kernel(size, size**-0.5, *refs),
        grid=(latents,),
        in_specs=[block(triple), block(2 * width)],
        out_specs=[block(width), pl.BlockSpec((None, rows, heads), lambda at: (at, 0, 0))],
        out_shape=[
            jax.ShapeDtypeStruct((chips, latents, tokens, width), LOW),
            jax.ShapeDtypeStruct((latents, rows, heads), FULL),
        ],
        compiler_params=pltpu.CompilerParams(vmem_limit_bytes=VMEM_LIMIT),
        cost_estimate=pl.CostEstimate(
            flops=8 * latents * rows * rows * width,
            bytes_accessed=6 * 2 * latents * rows * width,
            transcendentals=2 * latents * heads * rows * rows,
        ),
        name="attention_forward",
    )(own, other)


def attend_back_kernel(
    size, factor, own_ref, other_ref, grad_ref, log_ref, query_ref, kv_own_ref, kv_other_ref
):
    chips, tokens, triple = own_ref.shape
    width = triple // 3
    rows = chips * tokens
    own = own_ref[...].reshape(rows, triple)
    other = other_ref[...].reshape(rows, 2 * width)
    grad = grad_ref[...].reshape(rows, width)
    query_grads, key_own, value_own, key_other, value_other = [], [], [], [], []
    for head in range(width // size):
        lo, hi = head * size, (head + 1) * size
        queries = own[:, lo:hi] * jnp.asarray(factor, LOW)
        upstream = grad[:, lo:hi]
        logsum = log_ref[:, head : head + 1]
        keys_a = own[:, width + lo : width + hi]
        keys_b = other[:, lo:hi]
        prob_a = jnp.exp(dot_nt(queries, keys_a) - logsum)
        prob_b = jnp.exp(dot_nt(queries, keys_b) - logsum)
        grad_a = dot_nt(upstream, own[:, 2 * width + lo : 2 * width + hi])
        grad_b = dot_nt(upstream, other[:, width + lo : width + hi])
        terms = jnp.sum(prob_a * grad_a, axis=-1, keepdims=True)
        terms = terms + jnp.sum(prob_b * grad_b, axis=-1, keepdims=True)
        score_a = (prob_a * (grad_a - terms)).astype(LOW)
        score_b = (prob_b * (grad_b - terms)).astype(LOW)
        query_grads.append((dot(score_a, keys_a) + dot(score_b, keys_b)) * factor)
        key_own.append(dot_tn(score_a, queries))
        key_other.append(dot_tn(score_b, queries))
        value_own.append(dot_tn(prob_a.astype(LOW), upstream))
        value_other.append(dot_tn(prob_b.astype(LOW), upstream))
    query_ref[...] = (
        jnp.concatenate(query_grads, axis=1).astype(LOW).reshape(chips, tokens, width)
    )
    kv_own_ref[...] = jnp.concatenate(key_own + value_own, axis=1).reshape(
        chips, tokens, 2 * width
    )
    kv_other_ref[...] = jnp.concatenate(key_other + value_other, axis=1).reshape(
        chips, tokens, 2 * width
    )


def attend_back(own, other, grad, logsum, size):
    chips, latents, tokens, triple = own.shape
    width = triple // 3
    heads = width // size
    rows = chips * tokens

    def block(columns):
        return pl.BlockSpec((chips, None, tokens, columns), lambda at: (0, at, 0, 0))

    def shape(columns, dtype):
        return jax.ShapeDtypeStruct((chips, latents, tokens, columns), dtype)

    return pl.pallas_call(
        lambda *refs: attend_back_kernel(size, size**-0.5, *refs),
        grid=(latents,),
        in_specs=[
            block(triple),
            block(2 * width),
            block(width),
            pl.BlockSpec((None, rows, heads), lambda at: (at, 0, 0)),
        ],
        out_specs=[block(width), block(2 * width), block(2 * width)],
        out_shape=[shape(width, LOW), shape(2 * width, FULL), shape(2 * width, FULL)],
        compiler_params=pltpu.CompilerParams(vmem_limit_bytes=VMEM_LIMIT),
        cost_estimate=pl.CostEstimate(
            flops=20 * latents * rows * rows * width,
            bytes_accessed=26 * latents * rows * width,
            transcendentals=2 * latents * heads * rows * rows,
        ),
        name="attention_backward",
    )(own, other, grad, logsum)


def spread_plane(unit, x_first):
    if x_first:
        over_x = swap(unit, x=1)
        pair = jnp.concatenate([unit, over_x], axis=1)
        far = swap(pair, y=1)
        width = unit.shape[1]
        quad = jnp.concatenate([unit, far[:, :width], over_x, far[:, width:]], axis=1)
    else:
        pair = jnp.concatenate([unit, swap(unit, y=1)], axis=1)
        quad = jnp.concatenate([pair, swap(pair, x=1)], axis=1)
    return (quad, swap(quad, core=1))


def fetch_weight(place, shard, x_first):
    whole = place.gather_dp(shard)
    return spread_plane(whole.reshape(-1, shard.shape[1]), x_first)


def collect_grad(place, own_terms, other_terms, x_first):
    width = own_terms.shape[1] // 4
    quad = own_terms + swap(other_terms.astype(LOW), core=1).astype(FULL)
    units = [quad[:, at * width : (at + 1) * width] for at in range(4)]
    if x_first:
        sent = jnp.concatenate([units[1], units[3]], axis=1).astype(LOW)
        pair = jnp.concatenate([units[0], units[2]], axis=1) + swap(sent, y=1).astype(FULL)
        unit = pair[:, :width] + swap(pair[:, width:].astype(LOW), x=1).astype(FULL)
    else:
        pair = quad[:, : 2 * width] + swap(quad[:, 2 * width :].astype(LOW), x=1).astype(FULL)
        unit = pair[:, :width] + swap(pair[:, width:].astype(LOW), y=1).astype(FULL)
    return place.scatter_dp(unit.reshape(place.n_dp, -1, width), LOW)


def spread_ctx(place, unit):
    over_x = swap(unit, x=1)
    far = swap(jnp.stack([unit, over_x]), core=1)
    return unrelate([unit, far[0], over_x, far[1]], place.ctx)


def to_chips(place, blocks):
    arrived = []
    for at, (x, y) in enumerate(CHIPS):
        block = jnp.where(place.x ^ x == 0, blocks[y][0], blocks[y][1])
        arrived.append(block if at == 0 else swap(block, x=x, y=y))
    return jnp.stack(arrived)


def from_chips(place, stacked):
    arrived = [
        stacked[at] if at == 0 else swap(stacked[at], x=x, y=y) for at, (x, y) in enumerate(CHIPS)
    ]
    by_group = []
    for y in range(2):
        near, far = arrived[y], arrived[2 + y]
        by_group.append(
            (jnp.where(place.x == 0, near, far), jnp.where(place.x == 0, far, near))
        )
    return by_group


def block_forward(place, resid, modulation, weights, biases, size):
    (attn_quads, up_quads, down_quads) = weights
    (query_bias, value_bias, proj_bias, up_bias, down_bias) = biases
    latents, tokens, width = resid.shape
    shift_one, scale_one, gate_one, shift_two, scale_two, gate_two = [
        modulation[:, at : at + 1, :] for at in range(6)
    ]
    (near, far) = attn_quads
    four = unrelate([near[:, :width], far[:, :width], near[:, width:], far[:, width:]], place.ctx)
    qkv_weight = jnp.concatenate(four[:3], axis=1)
    proj_weight = four[3]
    normed_one, scaling_one = normalize(resid)
    entry_one = (normed_one * (1.0 + scale_one) + shift_one).astype(LOW).reshape(-1, width)
    projected = dot(entry_one, qkv_weight)
    queries = (projected[:, :width] + query_bias).astype(LOW)
    keys = projected[:, width : 2 * width].astype(LOW)
    values = (projected[:, 2 * width :] + value_bias).astype(LOW)
    part = width // 4
    blocks = [
        [
            jnp.concatenate(
                [
                    member[:, (2 * rel + group) * part : (2 * rel + group + 1) * part]
                    for member in (queries, keys, values)
                ],
                axis=1,
            )
            for group in range(2)
        ]
        for rel in range(2)
    ]
    own = to_chips(place, blocks)
    other = swap(own[:, :, part:], core=1)
    own = own.reshape(4, latents, tokens, 3 * part)
    other = other.reshape(4, latents, tokens, 2 * part)
    attn_out, logsum = attend(own, other, size)
    pieces = from_chips(place, attn_out.reshape(4, latents * tokens, part))
    context = jnp.concatenate([*pieces[0], *pieces[1]], axis=1)
    attended = (dot_nt(context, proj_weight) + proj_bias).reshape(resid.shape)
    middle = resid + gate_one * attended
    normed_two, scaling_two = normalize(middle)
    entry_two = (normed_two * (1.0 + scale_two) + shift_two).astype(LOW).reshape(-1, width)
    hidden_pre = [dot(entry_two, up_quads[at]) + up_bias[at] for at in range(2)]
    hidden = [activation(member).astype(LOW) for member in hidden_pre]
    mlp_out = dot_nt(hidden[0], down_quads[0]) + dot_nt(hidden[1], down_quads[1])
    mlp_out = (mlp_out + down_bias).reshape(resid.shape)
    result = middle + gate_two * mlp_out
    saved = (
        normed_one,
        scaling_one,
        entry_one,
        own,
        other,
        logsum,
        context,
        attended,
        normed_two,
        scaling_two,
        entry_two,
        hidden_pre,
        hidden,
        mlp_out,
        qkv_weight,
        proj_weight,
    )
    return (result, saved)


def block_backward(place, upstream, modulation, weights, saved, size):
    (attn_quads, up_quads, down_quads) = weights
    (
        normed_one,
        scaling_one,
        entry_one,
        own,
        other,
        logsum,
        context,
        attended,
        normed_two,
        scaling_two,
        entry_two,
        hidden_pre,
        hidden,
        mlp_out,
        qkv_weight,
        proj_weight,
    ) = saved
    latents, tokens, width = upstream.shape
    part = width // 4
    shift_one, scale_one, gate_one, shift_two, scale_two, gate_two = [
        modulation[:, at : at + 1, :] for at in range(6)
    ]
    gate_two_grad = jnp.sum(upstream * mlp_out, axis=1)
    mlp_grad = (gate_two * upstream).astype(LOW).reshape(-1, width)
    down_bias_grad = jnp.sum(mlp_grad, axis=0, dtype=FULL)
    down_grad = [dot_tn(mlp_grad, member) for member in hidden]
    down_shard = collect_grad(place, down_grad[0], down_grad[1], True)
    pre_grad = []
    for at in range(2):
        unused_value, gelu_pull = jax.vjp(activation, hidden_pre[at])
        pre_grad.append(gelu_pull(dot(mlp_grad, down_quads[at]))[0].astype(LOW))
    up_bias_grad = [jnp.sum(member, axis=0, dtype=FULL) for member in pre_grad]
    up_grad = [dot_tn(entry_two, member) for member in pre_grad]
    up_shard = collect_grad(place, up_grad[0], up_grad[1], False)
    entry_two_grad = dot_nt(pre_grad[0], up_quads[0]) + dot_nt(pre_grad[1], up_quads[1])
    entry_two_grad = entry_two_grad.reshape(upstream.shape)
    scale_two_grad = jnp.sum(entry_two_grad * normed_two, axis=1)
    shift_two_grad = jnp.sum(entry_two_grad, axis=1)
    middle_grad = upstream + norm_back(entry_two_grad * (1.0 + scale_two), normed_two, scaling_two)
    gate_one_grad = jnp.sum(middle_grad * attended, axis=1)
    attended_grad = (gate_one * middle_grad).astype(LOW).reshape(-1, width)
    proj_bias_grad = jnp.sum(attended_grad, axis=0, dtype=FULL)
    context_grad = dot(attended_grad, proj_weight).astype(LOW)
    blocks = [
        [context_grad[:, (2 * rel + at) * part : (2 * rel + at + 1) * part] for at in range(2)]
        for rel in range(2)
    ]
    out_grad = to_chips(place, blocks).reshape(4, latents, tokens, part)
    query_part, kv_own, kv_other = attend_back(own, other, out_grad, logsum, size)
    kv_part = (kv_own + swap(kv_other, core=1)).astype(LOW)
    pieces = from_chips(
        place,
        jnp.concatenate([query_part, kv_part], axis=-1).reshape(4, latents * tokens, 3 * part),
    )
    ordered = [*pieces[0], *pieces[1]]
    triple = [
        jnp.concatenate([member[:, at * part : (at + 1) * part] for member in ordered], axis=1)
        for at in range(3)
    ]
    query_bias_grad = jnp.sum(triple[0], axis=0, dtype=FULL)
    value_bias_grad = jnp.sum(triple[2], axis=0, dtype=FULL)
    entry_one_grad = dot_nt(jnp.concatenate(triple, axis=1), qkv_weight).reshape(upstream.shape)
    scale_one_grad = jnp.sum(entry_one_grad * normed_one, axis=1)
    shift_one_grad = jnp.sum(entry_one_grad, axis=1)
    resid_grad = middle_grad + norm_back(
        entry_one_grad * (1.0 + scale_one), normed_one, scaling_one
    )
    rights = jnp.stack([*triple, context])
    terms = []
    for at in range(4):
        matrix = place.ctx ^ at
        left = jnp.where(matrix == 3, attended_grad, entry_one)
        terms.append(dot_tn(left, lax.dynamic_index_in_dim(rights, matrix, 0, keepdims=False)))
    attn_shard = collect_grad(
        place,
        jnp.concatenate([terms[0], terms[2]], axis=1),
        jnp.concatenate([terms[1], terms[3]], axis=1),
        False,
    )
    mod_grad = jnp.stack(
        [
            shift_one_grad,
            scale_one_grad,
            gate_one_grad,
            shift_two_grad,
            scale_two_grad,
            gate_two_grad,
        ],
        axis=1,
    )
    def halves(value):
        return jnp.concatenate(
            [
                jnp.where(place.y == 0, value[: width // 2], value[width // 2 :]),
                jnp.where(place.y == 0, value[width // 2 :], value[: width // 2]),
            ]
        )

    quarters = [member.reshape(2, 2, -1) for member in up_bias_grad]
    by_ctx = unrelate([quarters[0][0], quarters[1][0], quarters[0][1], quarters[1][1]], place.ctx)
    by_unit = jnp.stack(by_ctx, axis=1)
    up_bias_all = jnp.concatenate(
        [
            jnp.where(place.y == 0, by_unit[0], by_unit[1]).reshape(-1),
            jnp.where(place.y == 0, by_unit[1], by_unit[0]).reshape(-1),
        ]
    )
    bias_grad = jnp.concatenate(
        [halves(query_bias_grad), halves(value_bias_grad), proj_bias_grad, up_bias_all, down_bias_grad]
    )
    return (resid_grad, (attn_shard, up_shard, down_shard), mod_grad, bias_grad)


def local(
    mesh,
    latents_in,
    condition,
    out_grad,
    mod_weight,
    mod_bias,
    qkv_weight,
    qkv_bias,
    proj_weight,
    proj_bias,
    fc1_weight,
    fc1_bias,
    fc2_weight,
    fc2_bias,
):
    place = Place(mesh)
    n_dp = place.n_dp
    layers = mod_weight.shape[0]
    latents, ctx_tokens, width = latents_in.shape
    tokens = ctx_tokens // 2
    rows = width // n_dp
    heads = qkv_bias.shape[2]
    size = qkv_bias.shape[3] * n_dp
    quarter = fc1_weight.shape[2] // 4

    all_weights = []
    for layer in range(layers):
        attn = pick(place.ctx, [*[qkv_weight[layer, at] for at in range(3)], proj_weight[layer]])
        start = place.ctx * quarter
        up = lax.dynamic_slice_in_dim(fc1_weight[layer], start, quarter, 1)
        down = lax.dynamic_slice_in_dim(fc2_weight[layer], start, quarter, 1)
        all_weights.append(
            (
                fetch_weight(place, attn, False),
                fetch_weight(place, up, False),
                fetch_weight(place, down, True),
            )
        )

    members = (mod_bias, qkv_bias, proj_bias, fc1_bias, fc2_bias)
    flat = jnp.concatenate(
        [condition.reshape(-1), *[member.astype(FULL).reshape(-1) for member in members]]
    )
    everyone = place.gather_dp(flat)
    cond_all = everyone[:, : condition.size].reshape(n_dp * latents, width)
    bias_near = everyone[:, condition.size :]
    bias_both = jnp.stack([bias_near, swap(bias_near, y=1)])
    taken = []
    start = 0
    for member in members:
        taken.append(
            bias_both[:, :, start : start + member.size].reshape((2, n_dp) + member.shape)
        )
        start += member.size
    spans = mod_bias.shape[1]
    mod_bias_half = jnp.moveaxis(taken[0][0], 0, 2).reshape(layers, spans * width)
    qkv_bias_all = jnp.transpose(taken[1], (2, 3, 0, 4, 1, 5)).reshape(layers, 2, 2 * heads * size)
    proj_bias_all = jnp.moveaxis(taken[2][0], 0, 1).reshape(layers, width)
    fc1_all = jnp.transpose(taken[3], (2, 0, 3, 1, 4)).reshape(layers, 2, 4, quarter)
    fc2_bias_all = jnp.moveaxis(taken[4][0], 0, 1).reshape(layers, width)
    fc1_rel = jnp.stack(
        [
            lax.dynamic_index_in_dim(fc1_all, place.ctx ^ at, 2, keepdims=False)
            for at in range(4)
        ]
    )
    fc1_rel = fc1_rel.reshape(2, 2, layers, 2, quarter)

    silu_all = jax.nn.silu(cond_all)
    silu_rows = lax.dynamic_slice_in_dim(silu_all, place.z * rows, rows, 1)
    halfmod = jnp.einsum(
        "bd,lde->lbe", silu_rows, mod_weight.astype(FULL), precision=PRECISE
    ).reshape(layers, n_dp, latents, -1)
    halfmod = place.scatter_dp(jnp.moveaxis(halfmod, 1, 0), FULL) + mod_bias_half[:, None, :]
    farmod = swap(halfmod, y=1)
    modulation = jnp.concatenate(
        [jnp.where(place.y == 0, halfmod, farmod), jnp.where(place.y == 0, farmod, halfmod)],
        axis=-1,
    ).reshape(layers, latents, 2 * spans, width)

    token_start = place.y * tokens
    resid = lax.dynamic_slice_in_dim(latents_in, token_start, tokens, 1).astype(FULL)
    upstream = lax.dynamic_slice_in_dim(out_grad, token_start, tokens, 1).astype(FULL)
    saved_list = []
    for layer in range(layers):
        up_bias = [
            jnp.moveaxis(fc1_rel[:, core, layer], 0, 0).reshape(-1) for core in range(2)
        ]
        biases = (
            qkv_bias_all[layer, 0],
            qkv_bias_all[layer, 1],
            proj_bias_all[layer],
            up_bias,
            fc2_bias_all[layer],
        )
        resid, saved = block_forward(
            place, resid, modulation[layer], all_weights[layer], biases, size
        )
        saved_list.append(saved)

    def both_halves(value):
        other = swap(value, y=1)
        return jnp.concatenate(
            [jnp.where(place.y == 0, value, other), jnp.where(place.y == 0, other, value)], axis=1
        )

    block_out = both_halves(resid.astype(LOW))
    shards = [None] * layers
    mod_grads = [None] * layers
    bias_grads = [None] * layers
    for layer in reversed(range(layers)):
        upstream, shards[layer], mod_grads[layer], bias_grads[layer] = block_backward(
            place, upstream, modulation[layer], all_weights[layer], saved_list[layer], size
        )
    latents_grad = both_halves(upstream)

    mod_stack = jnp.stack(mod_grads)
    bias_stack = jnp.stack(bias_grads)
    vector = jnp.concatenate([mod_stack.reshape(-1), bias_stack.reshape(-1)])
    vectors = place.gather_dp(place.sum_plane(vector))
    mod_all = vectors[:, : mod_stack.size].reshape((n_dp,) + mod_stack.shape)
    mod_all = jnp.moveaxis(mod_all, 0, 1).reshape(layers, n_dp * latents, 2, -1)
    own_mod = lax.dynamic_index_in_dim(mod_all, place.y, 2, keepdims=False)
    mod_wgrad = jnp.einsum("bd,lbe->lde", silu_rows, own_mod, precision=PRECISE)
    mod_bsum = jnp.sum(own_mod, axis=1).reshape(layers, spans, n_dp, rows)
    mod_bgrad = lax.dynamic_index_in_dim(mod_bsum, place.z, 2, keepdims=False)
    cond_part = jnp.einsum("lbe,lde->bd", own_mod, mod_weight.astype(FULL), precision=PRECISE)
    cond_part = cond_part + swap(cond_part, y=1)
    cond_blocks = place.gather_dp(cond_part).reshape(n_dp, n_dp, latents, rows)
    cond_sum = lax.dynamic_index_in_dim(cond_blocks, place.z, 1, keepdims=False)
    cond_sum = jnp.moveaxis(cond_sum, 0, 1).reshape(latents, width)
    unused_value, silu_pull = jax.vjp(jax.nn.silu, condition)
    condition_grad = silu_pull(cond_sum)[0]

    bias_sum = jnp.sum(vectors[:, mod_stack.size :], axis=0).reshape(layers, -1)
    qkv_b = bias_sum[:, : 2 * width].reshape(layers, 2, 2, heads, n_dp, -1)
    qkv_b = lax.dynamic_index_in_dim(qkv_b, place.y, 2, keepdims=False)
    qkv_bgrad = lax.dynamic_index_in_dim(qkv_b, place.z, 3, keepdims=False)
    proj_bgrad = lax.dynamic_slice_in_dim(
        bias_sum[:, 2 * width : 3 * width], place.z * rows, rows, 1
    )
    fc1_b = bias_sum[:, 3 * width : -width].reshape((layers, 2, fc1_bias.shape[1], n_dp, -1))
    fc1_b = lax.dynamic_index_in_dim(fc1_b, place.y, 1, keepdims=False)
    fc1_bgrad = lax.dynamic_index_in_dim(fc1_b, place.z, 2, keepdims=False)
    fc2_bgrad = lax.dynamic_slice_in_dim(bias_sum[:, -width:], place.z * rows, rows, 1)

    qkv_wgrad, proj_wgrad, fc1_wgrad, fc2_wgrad = [], [], [], []
    for layer in range(layers):
        attn_units, up_units, down_units = [spread_ctx(place, member) for member in shards[layer]]
        qkv_wgrad.append(jnp.stack(attn_units[:3]))
        proj_wgrad.append(attn_units[3])
        fc1_wgrad.append(jnp.concatenate(up_units, axis=1))
        fc2_wgrad.append(jnp.concatenate(down_units, axis=1))
    return (
        block_out,
        latents_grad,
        condition_grad,
        mod_wgrad,
        mod_bgrad,
        jnp.stack(qkv_wgrad),
        qkv_bgrad,
        jnp.stack(proj_wgrad),
        proj_bgrad,
        jnp.stack(fc1_wgrad),
        fc1_bgrad,
        jnp.stack(fc2_wgrad),
        fc2_bgrad,
    )


def solution(mesh):
    placed = (
        P("dp", "ctx", None),
        P("dp", None),
        P("dp", "ctx", None),
        P(None, "dp", "tp"),
        P(None, "tp", "dp"),
        P(None, None, "dp", "tp"),
        P(None, None, "tp", "dp"),
        P(None, "dp", "tp"),
        P(None, "dp"),
        P(None, "dp", "tp"),
        P(None, "tp", "dp"),
        P(None, "dp", "tp"),
        P(None, "dp"),
    )
    outs = (
        P("dp", "ctx", None),
        P("dp", "ctx", None),
        P("dp", None),
        P(None, "dp", "tp"),
        P(None, "tp", "dp"),
        P(None, None, "dp", "tp"),
        P(None, None, "tp", "dp"),
        P(None, "dp", "tp"),
        P(None, "dp"),
        P(None, "dp", "tp"),
        P(None, "tp", "dp"),
        P(None, "dp", "tp"),
        P(None, "dp"),
    )
    return jax.shard_map(
        lambda *arrays: local(mesh, *arrays),
        mesh=mesh,
        in_specs=placed,
        out_specs=outs,
        check_vma=False,
    )
```

time: 2620 us -> 1050 us (0.40)
  waiting for transfers between devices: 1790 us -> 381 us
  matrix products: 383 us -> 95.1 us
  blocking collectives: 198 us -> 0 us
  starting transfers between devices: 3.28 us -> 148 us
  other arithmetic: 90.6 us -> 170 us
  Pallas kernels: 0 us -> 62.1 us
  local copies, waits for them, and re-layouts: 135 us -> 172 us
    reduce_scatter x12 -> x0, waiting for transfers between devices: 670 us -> none  [the longest x2 253 us: reduce_grads(): lax.psum_scatter(mod_wgrad, 'dp', scatter_dimension=0, tiled=True)]
    psum x8 -> x0, waiting for transfers between devices: 573 us -> none  [the longest x7 399 us: branch_reduce(): return lax.psum(part, 'tp')]
    ppermute x0 -> x132, waiting for transfers between devices: none -> 381 us  [the longest x84 322 us: swap(): return lax.ppermute(value, PLANE, [(at, at ^ mask) for at in range(8)])]
    all_gather x12 -> x0, waiting for transfers between devices: 363 us -> none  [the longest x2 103 us: fetch_weights(): lax.all_gather(mod_weight, 'dp', axis=0, tiled=True)]
    dot_general x42 -> x43, matrix products: 383 us -> 95.1 us  [the longest x16 37.8 us: dot_tn(): lax.dot_general(left, right, (((0,), (0,)), ((), ())), preferred_element_...]
    unnamed x48 -> x0, waiting for transfers between devices: 179 us -> none
    ppermute x0 -> x132, starting transfers between devices: none -> 148 us  [the longest x84 75.1 us: swap(): return lax.ppermute(value, PLANE, [(at, at ^ mask) for at in range(8)])]
    all_gather x10 -> x0, blocking collectives: 132 us -> none  [the longest x2 36.7 us: fetch_weights(): lax.all_gather(mod_bias, 'dp', axis=1, tiled=True)]
  transfers between devices with their start and end apart: 40 -> 132, of which waited for: 31 -> 52; matrix products, arithmetic and copies ran while one was open for 17% -> 36% of each run, Pallas kernels for 0% -> 6%
where the time goes in v1:
time: 1050 us; the launch traced here: 1030 us
  waiting for transfers between devices  381 us (36%)
  local copies, waits for them, and re-layouts  172 us (16%)
  other arithmetic  170 us (16%)
  starting transfers between devices  148 us (14%)
  matrix products  95.1 us (9%)
  Pallas kernels  62.1 us (6%)
    ppermute x84, waiting for transfers between devices, swap(): return lax.ppermute(value, PLANE, [(at, at ^ mask) for at in range(8)])  322 us
    ppermute x84, starting transfers between devices, swap(): return lax.ppermute(value, PLANE, [(at, at ^ mask) for at in range(8)])  75.1 us
    ppermute x48, starting transfers between devices, swap_dp(): return lax.ppermute(value, 'dp', [(at, at ^ mask) for at in range(count)])  72.8 us
    ppermute x48, waiting for transfers between devices, swap_dp(): return lax.ppermute(value, 'dp', [(at, at ^ mask) for at in range(count)])  59.4 us
    unnamed x535, local copies, waits for them, and re-layouts  48.2 us
    dot_general x16, matrix products, dot_tn(): lax.dot_general(left, right, (((0,), (0,)), ((), ())), preferred_element_...  37.8 us
    pallas_call x2, Pallas kernels, attend_back(): pl.pallas_call(lambda *refs: attend_back_kernel(size, size ** (-0.5), *re...  37.6 us
    dot_general x12, matrix products, dot_nt(): lax.dot_general(left, right, (((1,), (1,)), ((), ())), preferred_element_...  25.9 us
  transfers between devices with their start and end apart: 132, of which 52 were waited for; matrix products, arithmetic and copies ran while one was open for 36% of the time, Pallas kernels for 6%

profile of v1, /device:TPU:0, one launch (start us, length us, event | category | flops | bytes accessed | tf_op | source)
XLA Modules:
  0.0 1033.2 jit_solution(912843909481813797)
XLA Ops:
  83.6 10.9 %collective-permute-done.11 = bf16[768,768]{1,0:T(8,128)(2,1)} collective-permute-done((bf16[768,768]{1,0:T(8,128)(2,1)}, bf16[768,768]{1,0:T(8,128)(2,1)}, u32[]{:S(2)}, u32[]{:S(2)}) %collective-permute-start.11) | collective-permute-done | bytes 1179680 | tf_op jit(solution)/shard_map/ppermute | solution.py:19
  116.3 14.5 %collective-permute-done.47 = bf16[192,384]{1,0:T(8,128)(2,1)S(1)} collective-permute-done((bf16[192,384]{1,0:T(8,128)(2,1)S(1)}, bf16[192,384]{1,0:T(8,128)(2,1)S(1)}, u32[]{:S(2)}, u32[]{:S(2)}) %collective-permute-start.47) | collective-permute-done | bytes 147488 | tf_op jit(solution)/shard_map/ppermute | solution.py:23
  151.0 9.8 collective-permute-done.24
  174.8 14.9 %collective-permute-done.37 = bf16[768,768]{1,0:T(8,128)(2,1)S(1)} collective-permute-done((bf16[768,768]{1,0:T(8,128)(2,1)S(1)}, bf16[768,768]{1,0:T(8,128)(2,1)S(1)}, u32[]{:S(2)}, u32[]{:S(2)}) %collective-permute-start.37) | collective-permute-done | bytes 1179680 | tf_op jit(solution)/shard_map/ppermute | solution.py:19
  204.7 29.9 %collective-permute-done.16 = bf16[384,576]{1,0:T(8,128)(2,1)S(1)} collective-permute-done((bf16[384,576]{1,0:T(8,128)(2,1)S(1)}, bf16[384,576]{1,0:T(8,128)(2,1)S(1)}, u32[]{:S(2)}, u32[]{:S(2)}) %collective-permute-start.16) | collective-permute-done | bytes 442400 | tf_op jit(solution)/shard_map/ppermute | solution.py:19
  247.9 12.5 %attention_forward.2 = (bf16[4,3,128,192]{3,2,1,0:T(8,128)(2,1)}, f32[3,512,3]{2,1,0:T(8,128)}) custom-call(bf16[4,3,128,576]{3,2,1,0:T(8,128)(2,1)} %pad_maximum_fusion.15.refs_0_, bf16[4,3,128,384]{3,2,1,0:T(8,128)(2,1)} %bitcast.911), custom_call_target="tpu_custom_call" | custom-call | flops 1207959552 | bytes 3538944 | tf_op jit(solution)/shard_map/attention_forward/pallas_call | solution.py:131
  269.1 8.6 collective-permute-done.20
  315.2 12.5 %collective-permute-done.39 = bf16[384,576]{1,0:T(8,128)(2,1)S(1)} collective-permute-done((bf16[384,576]{1,0:T(8,128)(2,1)S(1)}, bf16[384,576]{1,0:T(8,128)(2,1)S(1)}, u32[]{:S(2)}, u32[]{:S(2)}) %collective-permute-start.39) | collective-permute-done | bytes 442400 | tf_op jit(solution)/shard_map/ppermute | solution.py:19
  340.7 10.8 %collective-permute-done.55 = bf16[768,768]{1,0:T(8,128)(2,1)} collective-permute-done((bf16[768,768]{1,0:T(8,128)(2,1)}, bf16[768,768]{1,0:T(8,128)(2,1)}, u32[]{:S(2)}, u32[]{:S(2)}) %collective-permute-start.55) | collective-permute-done | bytes 1179680 | tf_op jit(solution)/shard_map/ppermute | solution.py:19
  355.9 12.0 %attention_forward.3 = (bf16[4,3,128,192]{3,2,1,0:T(8,128)(2,1)}, f32[3,512,3]{2,1,0:T(8,128)}) custom-call(bf16[4,3,128,576]{3,2,1,0:T(8,128)(2,1)} %pad_maximum_fusion.16.refs_0_, bf16[4,3,128,384]{3,2,1,0:T(8,128)(2,1)} %bitcast.89.refs_1_), custom_call_target="tpu_custom_call" | custom-call | flops 1207959552 | bytes 3538944 | tf_op jit(solution)/shard_map/attention_forward/pallas_call | solution.py:131
  429.9 18.8 %attention_backward.2 = (bf16[4,3,128,192]{3,2,1,0:T(8,128)(2,1)}, f32[4,3,128,384]{3,2,1,0:T(8,128)}, f32[4,3,128,384]{3,2,1,0:T(8,128)}) custom-call(bf16[4,3,128,576]{3,2,1,0:T(8,128)(2,1)} %pad_maximum_fusion.16.refs_0_, bf16[4,3,128,384]{3,2,1,0:T(8,128)(2,1)} %bitcast.89.refs_1_, bf16[4,3,128,192]{3,2,1,0:T(8,128)(2,1)} %pad_maximum_fusion.37.refs_2_, ...), custom_call_target="tpu_custom_call" | custom-call | flops 3019898880 | bytes 7667712 | tf_op jit(solution)/shard_map/attention_backward/pallas_call | solution.py:203
  487.0 22.7 %collective-permute-done.63 = bf16[384,576]{1,0:T(8,128)(2,1)S(1)} collective-permute-done((bf16[384,576]{1,0:T(8,128)(2,1)S(1)}, bf16[384,576]{1,0:T(8,128)(2,1)S(1)}, u32[]{:S(2)}, u32[]{:S(2)}) %collective-permute-start.63) | collective-permute-done | bytes 442400 | tf_op jit(solution)/shard_map/ppermute | solution.py:19
  510.6 9.9 collective-permute-done.65
  520.5 9.9 collective-permute-done.64
  602.4 7.7 collective-permute-done.110
  623.2 8.6 collective-permute-done.112
  648.0 6.9 collective-permute-done.67
  670.9 18.8 %attention_backward.3 = (bf16[4,3,128,192]{3,2,1,0:T(8,128)(2,1)}, f32[4,3,128,384]{3,2,1,0:T(8,128)}, f32[4,3,128,384]{3,2,1,0:T(8,128)}) custom-call(bf16[4,3,128,576]{3,2,1,0:T(8,128)(2,1)} %pad_maximum_fusion.15.refs_0_, bf16[4,3,128,384]{3,2,1,0:T(8,128)(2,1)} %bitcast.912, bf16[4,3,128,192]{3,2,1,0:T(8,128)(2,1)} %pad_maximum_fusion.38.refs_2_, ...), custom_call_target="tpu_custom_call" | custom-call | flops 3019898880 | bytes 7667712 | tf_op jit(solution)/shard_map/attention_backward/pallas_call | solution.py:203
  720.9 44.7 %collective-permute-done.70 = bf16[384,576]{1,0:T(8,128)(2,1)S(1)} collective-permute-done((bf16[384,576]{1,0:T(8,128)(2,1)S(1)}, bf16[384,576]{1,0:T(8,128)(2,1)S(1)}, u32[]{:S(2)}, u32[]{:S(2)}) %collective-permute-start.70) | collective-permute-done | bytes 442400 | tf_op jit(solution)/shard_map/ppermute | solution.py:19
  768.3 8.2 collective-permute-done.72
  776.5 10.3 collective-permute-done.71
  898.1 22.5 %collective-permute-done.94 = bf16[768,384]{0,1:T(8,128)(2,1)} collective-permute-done((bf16[768,384]{0,1:T(8,128)(2,1)}, bf16[768,384]{0,1:T(8,128)(2,1)}, u32[]{:S(2)}, u32[]{:S(2)}) %collective-permute-start.94) | collective-permute-done | bytes 589856 | tf_op jit(solution)/shard_map/ppermute | solution.py:19
  964.0 12.4 %collective-permute-done.106 = f32[192,384]{1,0:T(8,128)S(1)} collective-permute-done((f32[192,384]{1,0:T(8,128)S(1)}, f32[192,384]{1,0:T(8,128)S(1)}, u32[]{:S(2)}, u32[]{:S(2)}) %collective-permute-start.106) | collective-permute-done | bytes 294944 | tf_op jit(solution)/shard_map/ppermute | solution.py:19
  988.0 11.8 %collective-permute-done.86 = bf16[768,384]{0,1:T(8,128)(2,1)S(1)} collective-permute-done((bf16[768,384]{0,1:T(8,128)(2,1)S(1)}, bf16[768,384]{0,1:T(8,128)(2,1)S(1)}, u32[]{:S(2)}, u32[]{:S(2)}) %collective-permute-start.86) | collective-permute-done | bytes 589856 | tf_op jit(solution)/shard_map/ppermute | solution.py:19
  (1173 shorter events, 678.6 us)
Async XLA Ops:
  33.3 68.2 %collective-permute-start.22 = (bf16[192,384]{1,0:T(8,128)(2,1)}, bf16[192,384]{1,0:T(8,128)(2,1)}, u32[]{:S(2)}, u32[]{:S(2)}) collective-permute-start(bf16[192,384]{1,0:T(8,128)(2,1)} %dynamic-slice_bitcast_fusion.3), channel_id=1, source_target_pairs={{0,16},{8,24},{16,0},{24,8},{1,17},{9,25},{17,1},{25,9},{2,18},{10... | collective-permute-start | bytes 442376 | tf_op jit(solution)/shard_map/ppermute | solution.py:23
  35.8 67.1 %collective-permute-start.23 = (bf16[192,384]{1,0:T(8,128)(2,1)}, bf16[192,384]{1,0:T(8,128)(2,1)}, u32[]{:S(2)}, u32[]{:S(2)}) collective-permute-start(bf16[192,384]{1,0:T(8,128)(2,1)} %dynamic-slice_bitcast_fusion.3), channel_id=1, source_target_pairs={{0,24},{8,16},{16,8},{24,0},{1,25},{9,17},{17,9},{25,1},{2,26},{10... | collective-permute-start | bytes 442376 | tf_op jit(solution)/shard_map/ppermute | solution.py:23
  97.5 64.9 %collective-permute-start.12 = (bf16[768,1536]{1,0:T(8,128)(2,1)}, bf16[768,1536]{1,0:T(8,128)(2,1)}, u32[]{:S(2)}, u32[]{:S(2)}) collective-permute-start(bf16[768,1536]{1,0:T(8,128)(2,1)} %pad_maximum_fusion.2), channel_id=1, source_target_pairs={{0,2},{1,3},{2,0},{3,1},{4,6},{5,7},{6,4},{7,5},{8,10},{9,11},{10,... | collective-permute-start | bytes 7077896 | tf_op jit(solution)/shard_map/ppermute | solution.py:19
  142.1 50.7 %collective-permute-start.53 = (bf16[192,384]{1,0:T(8,128)(2,1)S(1)}, bf16[192,384]{1,0:T(8,128)(2,1)S(1)}, u32[]{:S(2)}, u32[]{:S(2)}) collective-permute-start(bf16[192,384]{1,0:T(8,128)(2,1)S(1)} %copy-done.194), channel_id=1, source_target_pairs={{0,24},{8,16},{16,8},{24,0},{1,25},{9,17},{17,9},{25,1},{2,26},{10... | collective-permute-start | bytes 442376 | tf_op jit(solution)/shard_map/ppermute | solution.py:23
  189.7 51.0 %collective-permute-start.25 = (bf16[768,768]{1,0:T(8,128)(2,1)S(1)}, bf16[768,768]{1,0:T(8,128)(2,1)S(1)}, u32[]{:S(2)}, u32[]{:S(2)}) collective-permute-start(bf16[768,768]{1,0:T(8,128)(2,1)S(1)} %pad_maximum_fusion.29), channel_id=1, source_target_pairs={{0,4},{1,5},{2,6},{3,7},{4,0},{5,1},{6,2},{7,3},{8,12},{9,13},{10,... | collective-permute-start | bytes 3538952 | tf_op jit(solution)/shard_map/ppermute | solution.py:19
  192.8 50.1 %collective-permute-start.30 = (bf16[768,768]{1,0:T(8,128)(2,1)S(1)}, bf16[768,768]{1,0:T(8,128)(2,1)S(1)}, u32[]{:S(2)}, u32[]{:S(2)}) collective-permute-start(bf16[768,768]{1,0:T(8,128)(2,1)S(1)} %pad_maximum_fusion.30), channel_id=1, source_target_pairs={{0,1},{1,0},{2,3},{3,2},{4,5},{5,4},{6,7},{7,6},{8,9},{9,8},{10,11... | collective-permute-start | bytes 3538952 | tf_op jit(solution)/shard_map/ppermute | solution.py:19
  194.0 69.9 %collective-permute-start.38 = (bf16[768,1536]{1,0:T(8,128)(2,1)}, bf16[768,1536]{1,0:T(8,128)(2,1)}, u32[]{:S(2)}, u32[]{:S(2)}) collective-permute-start(bf16[768,1536]{1,0:T(8,128)(2,1)} %pad_maximum_fusion.5), channel_id=1, source_target_pairs={{0,2},{1,3},{2,0},{3,1},{4,6},{5,7},{6,4},{7,5},{8,10},{9,11},{10,... | collective-permute-start | bytes 7077896 | tf_op jit(solution)/shard_map/ppermute | solution.py:19
  234.7 70.4 %collective-permute-start.54 = (bf16[768,384]{1,0:T(8,128)(2,1)S(1)}, bf16[768,384]{1,0:T(8,128)(2,1)}, u32[]{:S(2)}, u32[]{:S(2)}) collective-permute-start(bf16[768,384]{1,0:T(8,128)(2,1)S(1)} %bitcast.740), channel_id=1, source_target_pairs={{0,4},{1,5},{2,6},{3,7},{4,0},{5,1},{6,2},{7,3},{8,12},{9,13},{10,... | collective-permute-start | bytes 1769480 | tf_op jit(solution)/shard_map/ppermute | solution.py:19
  240.8 97.5 %collective-permute-start.50 = (bf16[768,768]{1,0:T(8,128)(2,1)}, bf16[768,768]{1,0:T(8,128)(2,1)}, u32[]{:S(2)}, u32[]{:S(2)}) collective-permute-start(bf16[768,768]{1,0:T(8,128)(2,1)} %pad_maximum_fusion.32), channel_id=1, source_target_pairs={{0,4},{1,5},{2,6},{3,7},{4,0},{5,1},{6,2},{7,3},{8,12},{9,13},{10,... | collective-permute-start | bytes 3538952 | tf_op jit(solution)/shard_map/ppermute | solution.py:19
  410.9 52.0 %collective-permute-start.108 = (bf16[768,1536]{1,0:T(8,128)(2,1)}, bf16[768,1536]{1,0:T(8,128)(2,1)}, u32[]{:S(2)}, u32[]{:S(2)}) collective-permute-start(bf16[768,1536]{1,0:T(8,128)(2,1)} %convolution_convert_fusion.2), channel_id=1, source_target_pairs={{0,2},{1,3},{2,0},{3,1},{4,6},{5,7},{6,4},{7,5},{8,10},{9,11},{10,... | collective-permute-start | bytes 7077896 | tf_op jit(solution)/shard_map/ppermute | solution.py:19
  410.9 60.8 %collective-permute-start.124 = (bf16[768,1536]{1,0:T(8,128)(2,1)}, bf16[768,1536]{1,0:T(8,128)(2,1)}, u32[]{:S(2)}, u32[]{:S(2)}) collective-permute-start(bf16[768,1536]{1,0:T(8,128)(2,1)} %convolution_convert_fusion), channel_id=1, source_target_pairs={{0,2},{1,3},{2,0},{3,1},{4,6},{5,7},{6,4},{7,5},{8,10},{9,11},{10,... | collective-permute-start | bytes 7077896 | tf_op jit(solution)/shard_map/ppermute | solution.py:19
  470.2 122.4 %collective-permute-start.109 = (bf16[768,768]{1,0:T(8,128)(2,1)}, bf16[768,768]{1,0:T(8,128)(2,1)}, u32[]{:S(2)}, u32[]{:S(2)}) collective-permute-start(bf16[768,768]{1,0:T(8,128)(2,1)} %slice.1518), channel_id=1, source_target_pairs={{0,4},{1,5},{2,6},{3,7},{4,0},{5,1},{6,2},{7,3},{8,12},{9,13},{10,... | collective-permute-start | bytes 3538952 | tf_op jit(solution)/shard_map/ppermute | solution.py:19
  481.3 115.9 %collective-permute-start.125 = (bf16[768,768]{1,0:T(8,128)(2,1)}, bf16[768,768]{1,0:T(8,128)(2,1)}, u32[]{:S(2)}, u32[]{:S(2)}) collective-permute-start(bf16[768,768]{1,0:T(8,128)(2,1)} %pad_maximum_fusion.36), channel_id=1, source_target_pairs={{0,1},{1,0},{2,3},{3,2},{4,5},{5,4},{6,7},{7,6},{8,9},{9,8},{10,11... | collective-permute-start | bytes 3538952 | tf_op jit(solution)/shard_map/ppermute | solution.py:19
  589.5 104.2 %collective-permute-start.100 = (bf16[768,1536]{1,0:T(8,128)(2,1)}, bf16[768,1536]{1,0:T(8,128)(2,1)}, u32[]{:S(2)}, u32[]{:S(2)}) collective-permute-start(bf16[768,1536]{1,0:T(8,128)(2,1)} %convolution_convert_fusion.3), channel_id=1, source_target_pairs={{0,2},{1,3},{2,0},{3,1},{4,6},{5,7},{6,4},{7,5},{8,10},{9,11},{10,... | collective-permute-start | bytes 7077896 | tf_op jit(solution)/shard_map/ppermute | solution.py:19
  597.1 105.0 %collective-permute-start.92 = (bf16[768,1536]{0,1:T(8,128)(2,1)}, bf16[768,1536]{0,1:T(8,128)(2,1)}, u32[]{:S(2)}, u32[]{:S(2)}) collective-permute-start(bf16[768,1536]{0,1:T(8,128)(2,1)} %pad_maximum_fusion.12), channel_id=1, source_target_pairs={{0,2},{1,3},{2,0},{3,1},{4,6},{5,7},{6,4},{7,5},{8,10},{9,11},{10,... | collective-permute-start | bytes 7077896 | tf_op jit(solution)/shard_map/ppermute | solution.py:19
  647.0 59.3 %collective-permute-start.116 = (bf16[768,1536]{1,0:T(8,128)(2,1)}, bf16[768,1536]{1,0:T(8,128)(2,1)}, u32[]{:S(2)}, u32[]{:S(2)}) collective-permute-start(bf16[768,1536]{1,0:T(8,128)(2,1)} %convolution_convert_fusion.1), channel_id=1, source_target_pairs={{0,2},{1,3},{2,0},{3,1},{4,6},{5,7},{6,4},{7,5},{8,10},{9,11},{10,... | collective-permute-start | bytes 7077896 | tf_op jit(solution)/shard_map/ppermute | solution.py:19
  700.8 129.9 %collective-permute-start.101 = (bf16[768,768]{1,0:T(8,128)(2,1)}, bf16[768,768]{1,0:T(8,128)(2,1)}, u32[]{:S(2)}, u32[]{:S(2)}) collective-permute-start(bf16[768,768]{1,0:T(8,128)(2,1)} %slice.1519), channel_id=1, source_target_pairs={{0,4},{1,5},{2,6},{3,7},{4,0},{5,1},{6,2},{7,3},{8,12},{9,13},{10,... | collective-permute-start | bytes 3538952 | tf_op jit(solution)/shard_map/ppermute | solution.py:19
  705.4 130.6 %collective-permute-start.93 = (bf16[768,768]{0,1:T(8,128)(2,1)}, bf16[768,768]{0,1:T(8,128)(2,1)}, u32[]{:S(2)}, u32[]{:S(2)}) collective-permute-start(bf16[768,768]{0,1:T(8,128)(2,1)} %slice.1520), channel_id=1, source_target_pairs={{0,4},{1,5},{2,6},{3,7},{4,0},{5,1},{6,2},{7,3},{8,12},{9,13},{10,... | collective-permute-start | bytes 3538952 | tf_op jit(solution)/shard_map/ppermute | solution.py:19
  714.6 51.0 %collective-permute-start.70 = (bf16[384,576]{1,0:T(8,128)(2,1)S(1)}, bf16[384,576]{1,0:T(8,128)(2,1)S(1)}, u32[]{:S(2)}, u32[]{:S(2)}) collective-permute-start(bf16[384,576]{1,0:T(8,128)(2,1)S(1)} %bitcast.861), channel_id=1, source_target_pairs={{0,4},{1,5},{2,6},{3,7},{4,0},{5,1},{6,2},{7,3},{8,12},{9,13},{10,... | collective-permute-start | bytes 1327112 | tf_op jit(solution)/shard_map/ppermute | solution.py:19
  716.8 124.1 %collective-permute-start.117 = (bf16[768,768]{1,0:T(8,128)(2,1)}, bf16[768,768]{1,0:T(8,128)(2,1)}, u32[]{:S(2)}, u32[]{:S(2)}) collective-permute-start(bf16[768,768]{1,0:T(8,128)(2,1)} %pad_maximum_fusion.35), channel_id=1, source_target_pairs={{0,1},{1,0},{2,3},{3,2},{4,5},{5,4},{6,7},{7,6},{8,9},{9,8},{10,11... | collective-permute-start | bytes 3538952 | tf_op jit(solution)/shard_map/ppermute | solution.py:19
  720.3 56.2 %collective-permute-start.72 = (bf16[384,576]{1,0:T(8,128)(2,1)S(1)}, bf16[384,576]{1,0:T(8,128)(2,1)S(1)}, u32[]{:S(2)}, u32[]{:S(2)}) collective-permute-start(bf16[384,576]{1,0:T(8,128)(2,1)S(1)} %bitcast.859), channel_id=1, source_target_pairs={{0,5},{1,4},{2,7},{3,6},{4,1},{5,0},{6,3},{7,2},{8,13},{9,12},{10,... | collective-permute-start | bytes 1327112 | tf_op jit(solution)/shard_map/ppermute | solution.py:19
  822.0 112.4 %collective-permute-start.84 = (bf16[768,1536]{0,1:T(8,128)(2,1)}, bf16[768,1536]{0,1:T(8,128)(2,1)}, u32[]{:S(2)}, u32[]{:S(2)}) collective-permute-start(bf16[768,1536]{0,1:T(8,128)(2,1)} %pad_maximum_fusion.10), channel_id=1, source_target_pairs={{0,2},{1,3},{2,0},{3,1},{4,6},{5,7},{6,4},{7,5},{8,10},{9,11},{10,... | collective-permute-start | bytes 7077896 | tf_op jit(solution)/shard_map/ppermute | solution.py:19
  840.9 53.7 %collective-permute-start.102 = (bf16[768,384]{1,0:T(8,128)(2,1)}, bf16[768,384]{1,0:T(8,128)(2,1)}, u32[]{:S(2)}, u32[]{:S(2)}) collective-permute-start(bf16[768,384]{1,0:T(8,128)(2,1)} %slice.1525), channel_id=1, source_target_pairs={{0,1},{1,0},{2,3},{3,2},{4,5},{5,4},{6,7},{7,6},{8,9},{9,8},{10,11... | collective-permute-start | bytes 1769480 | tf_op jit(solution)/shard_map/ppermute | solution.py:19
  882.9 47.5 %collective-permute-start.73 = (f32[3,128,768]{2,1,0:T(8,128)S(1)}, f32[3,128,768]{2,1,0:T(8,128)}, u32[]{:S(2)}, u32[]{:S(2)}) collective-permute-start(f32[3,128,768]{2,1,0:T(8,128)S(1)} %get-tuple-element.175), channel_id=1, source_target_pairs={{0,1},{1,0},{2,3},{3,2},{4,5},{5,4},{6,7},{7,6},{8,9},{9,8},{10,11... | collective-permute-start | bytes 3538952 | tf_op jit(solution)/shard_map/ppermute | solution.py:19
  (362 other events, 4277.9 us)

commit v2 on v1

v2 whole, which is shorter than its diff:
```python
import jax
import jax.numpy as jnp
from jax import lax
from jax.experimental import pallas as pl
from jax.experimental.pallas import tpu as pltpu
from jax.sharding import PartitionSpec as P

PRECISE = lax.Precision.HIGHEST
EPSILON = 1e-06
LOW = jnp.bfloat16
FULL = jnp.float32
CHIPS = ((0, 0), (0, 1), (1, 0), (1, 1))
PLANE = ("ctx", "tp")
VMEM_LIMIT = 56 * 1024 * 1024


def swap(value, x=0, core=0, y=0):
    mask = 4 * x + 2 * core + y
    return lax.ppermute(value, PLANE, [(at, at ^ mask) for at in range(8)])


def swap_dp(value, mask, count):
    return lax.ppermute(value, "dp", [(at, at ^ mask) for at in range(count)])


def pick(index, options):
    if len(options) == 1:
        return options[0]
    half = len(options) // 2
    low, high = pick(index % half, options[:half]), pick(index % half, options[half:])
    return jnp.where(index // half == 0, low, high)


def tie(value, after):
    if after is None:
        return value
    return lax.optimization_barrier((value, after))[0]


def unrelate(pieces, index):
    return [pick(index, [pieces[place ^ at] for at in range(len(pieces))]) for place in range(len(pieces))]


class Place:
    def __init__(self, mesh):
        self.n_dp = mesh.shape["dp"]
        self.z = lax.axis_index("dp")
        self.ctx = lax.axis_index("ctx")
        self.x = self.ctx // 2
        self.core = self.ctx % 2
        self.y = lax.axis_index("tp")
        self.direct = self.n_dp <= 4 and self.n_dp & (self.n_dp - 1) == 0

    def gather_dp(self, value):
        if not self.direct:
            return lax.all_gather(value, "dp")
        pieces = [value] + [swap_dp(value, mask, self.n_dp) for mask in range(1, self.n_dp)]
        return jnp.stack(unrelate(pieces, self.z))

    def scatter_dp(self, parts, dtype):
        if not self.direct:
            whole = jnp.stack([parts(at) for at in range(self.n_dp)]).astype(dtype)
            return lax.psum_scatter(whole, "dp", scatter_dimension=0).astype(FULL)
        total = parts(self.z)
        for mask in range(1, self.n_dp):
            part = parts(self.z ^ mask).astype(dtype)
            total = total + swap_dp(part, mask, self.n_dp).astype(FULL)
        return total

    def by_y(self, near, far):
        return (jnp.where(self.y == 0, near, far), jnp.where(self.y == 0, far, near))

    def unit_matrix(self):
        at = lax.broadcasted_iota(jnp.int32, (8, 8), 0)
        rel = lax.broadcasted_iota(jnp.int32, (8, 8), 1)
        flip_core = (at % 2) ^ self.core
        flip_x = (at // 2 % 2) ^ self.x
        flip_y = (at // 4) ^ self.y
        return (rel == 4 * flip_core + 2 * flip_x + flip_y).astype(FULL)


def normalize(field):
    centre = field - jnp.mean(field, axis=-1, keepdims=True)
    scaling = lax.rsqrt(jnp.mean(centre * centre, axis=-1, keepdims=True) + EPSILON)
    return (centre * scaling, scaling)


def norm_back(upstream, normed, scaling):
    first = jnp.mean(upstream, axis=-1, keepdims=True)
    second = jnp.mean(upstream * normed, axis=-1, keepdims=True)
    return scaling * (upstream - first - normed * second)


def activation(field):
    return jax.nn.gelu(field, approximate=True)


def dot(left, right):
    return jnp.dot(left, right, preferred_element_type=FULL)


def dot_nt(left, right):
    return lax.dot_general(left, right, (((1,), (1,)), ((), ())), preferred_element_type=FULL)


def dot_tn(left, right):
    return lax.dot_general(left, right, (((0,), (0,)), ((), ())), preferred_element_type=FULL)


def attend_kernel(size, factor, *refs):
    own_refs, other_refs, out_refs, log_ref = refs[:4], refs[4:8], refs[8:12], refs[12]
    tokens, triple = own_refs[0].shape
    width = triple // 3
    own = jnp.concatenate([ref[...] for ref in own_refs], axis=0)
    other = jnp.concatenate([ref[:, : 2 * width] for ref in other_refs], axis=0)
    outs = []
    for head in range(width // size):
        lo, hi = head * size, (head + 1) * size
        queries = own[:, 2 * width + lo : 2 * width + hi] * jnp.asarray(factor, LOW)
        score_a = dot_nt(queries, own[:, lo:hi])
        score_b = dot_nt(queries, other[:, lo:hi])
        highest = jnp.maximum(
            jnp.max(score_a, axis=-1, keepdims=True), jnp.max(score_b, axis=-1, keepdims=True)
        )
        exp_a = jnp.exp(score_a - highest)
        exp_b = jnp.exp(score_b - highest)
        total = jnp.sum(exp_a, axis=-1, keepdims=True) + jnp.sum(exp_b, axis=-1, keepdims=True)
        inverse = 1.0 / total
        out = dot((exp_a * inverse).astype(LOW), own[:, width + lo : width + hi])
        out = out + dot((exp_b * inverse).astype(LOW), other[:, width + lo : width + hi])
        outs.append(out)
        log_ref[:, head : head + 1] = highest + jnp.log(total)
    out = jnp.concatenate(outs, axis=1).astype(LOW)
    for at in range(4):
        out_refs[at][...] = out[at * tokens : (at + 1) * tokens]


def attend(own, other, size):
    latents, tokens, triple = own[0].shape
    width = triple // 3
    heads = width // size
    rows = 4 * tokens

    def block(columns):
        return pl.BlockSpec((None, tokens, columns), lambda at: (at, 0, 0))

    results = pl.pallas_call(
        lambda *refs: attend_kernel(size, size**-0.5, *refs),
        grid=(latents,),
        in_specs=[block(triple)] * 8,
        out_specs=[block(width)] * 4 + [pl.BlockSpec((None, rows, heads), lambda at: (at, 0, 0))],
        out_shape=[jax.ShapeDtypeStruct((latents, tokens, width), LOW)] * 4
        + [jax.ShapeDtypeStruct((latents, rows, heads), FULL)],
        compiler_params=pltpu.CompilerParams(vmem_limit_bytes=VMEM_LIMIT),
        cost_estimate=pl.CostEstimate(
            flops=8 * latents * rows * rows * width,
            bytes_accessed=14 * latents * rows * width,
            transcendentals=2 * latents * heads * rows * rows,
        ),
        name="attention_forward",
    )(*own, *other)
    return (results[:4], results[4])


def attend_back_kernel(size, factor, *refs):
    own_refs, other_refs, grad_refs, log_ref = refs[:4], refs[4:8], refs[8:12], refs[12]
    query_ref, kv_own_ref, kv_other_ref = refs[13:]
    tokens, triple = own_refs[0].shape
    width = triple // 3
    rows = 4 * tokens
    own = jnp.concatenate([ref[...] for ref in own_refs], axis=0)
    other = jnp.concatenate([ref[:, : 2 * width] for ref in other_refs], axis=0)
    grad = jnp.concatenate([ref[...] for ref in grad_refs], axis=0)
    query_grads, key_own, value_own, key_other, value_other = [], [], [], [], []
    for head in range(width // size):
        lo, hi = head * size, (head + 1) * size
        queries = own[:, 2 * width + lo : 2 * width + hi] * jnp.asarray(factor, LOW)
        upstream = grad[:, lo:hi]
        logsum = log_ref[:, head : head + 1]
        keys_a = own[:, lo:hi]
        keys_b = other[:, lo:hi]
        prob_a = jnp.exp(dot_nt(queries, keys_a) - logsum)
        prob_b = jnp.exp(dot_nt(queries, keys_b) - logsum)
        grad_a = dot_nt(upstream, own[:, width + lo : width + hi])
        grad_b = dot_nt(upstream, other[:, width + lo : width + hi])
        terms = jnp.sum(prob_a * grad_a, axis=-1, keepdims=True)
        terms = terms + jnp.sum(prob_b * grad_b, axis=-1, keepdims=True)
        score_a = (prob_a * (grad_a - terms)).astype(LOW)
        score_b = (prob_b * (grad_b - terms)).astype(LOW)
        query_grads.append((dot(score_a, keys_a) + dot(score_b, keys_b)) * factor)
        key_own.append(dot_tn(score_a, queries))
        key_other.append(dot_tn(score_b, queries))
        value_own.append(dot_tn(prob_a.astype(LOW), upstream))
        value_other.append(dot_tn(prob_b.astype(LOW), upstream))
    query_ref[...] = jnp.concatenate(query_grads, axis=1).astype(LOW).reshape(4, tokens, width)
    kv_own_ref[...] = jnp.concatenate(key_own + value_own, axis=1).reshape(4, tokens, 2 * width)
    kv_other_ref[...] = jnp.concatenate(key_other + value_other, axis=1).reshape(
        4, tokens, 2 * width
    )


def attend_back(own, other, grad, logsum, size):
    latents, tokens, triple = own[0].shape
    width = triple // 3
    heads = width // size
    rows = 4 * tokens

    def block(columns):
        return pl.BlockSpec((None, tokens, columns), lambda at: (at, 0, 0))

    def four(columns):
        return pl.BlockSpec((4, None, tokens, columns), lambda at: (0, at, 0, 0))

    def shape(columns, dtype):
        return jax.ShapeDtypeStruct((4, latents, tokens, columns), dtype)

    return pl.pallas_call(
        lambda *refs: attend_back_kernel(size, size**-0.5, *refs),
        grid=(latents,),
        in_specs=[block(triple)] * 8
        + [block(width)] * 4
        + [pl.BlockSpec((None, rows, heads), lambda at: (at, 0, 0))],
        out_specs=[four(width), four(2 * width), four(2 * width)],
        out_shape=[shape(width, LOW), shape(2 * width, FULL), shape(2 * width, FULL)],
        compiler_params=pltpu.CompilerParams(vmem_limit_bytes=VMEM_LIMIT),
        cost_estimate=pl.CostEstimate(
            flops=20 * latents * rows * rows * width,
            bytes_accessed=32 * latents * rows * width,
            transcendentals=2 * latents * heads * rows * rows,
        ),
        name="attention_backward",
    )(*own, *other, *grad, logsum)


class Weight:
    def __init__(self, unit, x_first):
        self.unit, self.x_first = unit, x_first

    def first(self, after=None):
        axis = "x" if self.x_first else "y"
        self.side = swap(tie(self.unit, after), **{axis: 1})

    def second(self, after=None):
        pair = jnp.concatenate([self.unit, self.side], axis=1)
        axis = "y" if self.x_first else "x"
        self.cross = swap(tie(pair, after), **{axis: 1})
        width = self.unit.shape[1]
        if self.x_first:
            parts = [self.unit, self.cross[:, :width], self.side, self.cross[:, width:]]
        else:
            parts = [pair, self.cross]
        self.near = jnp.concatenate(parts, axis=1)
        self.far = swap(self.near, core=1)

    def both(self):
        return (self.near, self.far)


class Grad:
    def __init__(self, near, far, width, x_first):
        self.near, self.width, self.x_first = near, width, x_first
        self.core = swap(far.astype(LOW), core=1)

    def term(self, unit):
        lo, hi = unit * self.width, (unit + 1) * self.width
        return self.near(lo, hi) + self.core[:, lo:hi].astype(FULL)

    def ready_first(self):
        if self.x_first:
            self.sent = jnp.concatenate(
                [self.term(1).astype(LOW), self.term(3).astype(LOW)], axis=1
            )
        else:
            lo, hi = 2 * self.width, 4 * self.width
            self.sent = (self.near(lo, hi) + self.core[:, lo:hi].astype(FULL)).astype(LOW)
        return self.sent

    def first(self, after=None):
        axis = "y" if self.x_first else "x"
        self.side = swap(tie(self.sent, after), **{axis: 1})

    def ready_second(self):
        sent = self.term(2 if self.x_first else 1) + self.side[:, self.width :].astype(FULL)
        self.sent = sent.astype(LOW)
        return self.sent

    def second(self, after=None):
        axis = "x" if self.x_first else "y"
        self.cross = swap(tie(self.sent, after), **{axis: 1})

    def unit(self):
        unit = self.term(0) + self.side[:, : self.width].astype(FULL)
        return unit + self.cross.astype(FULL)


def spread_ctx(place, unit):
    over_x = swap(unit, x=1)
    far = swap(jnp.stack([unit, over_x]), core=1)
    return unrelate([unit, far[0], over_x, far[1]], place.ctx)


def to_chips(place, blocks, after=None):
    arrived = []
    for at, (x, y) in enumerate(CHIPS):
        block = jnp.where(place.x ^ x == 0, blocks[y][0], blocks[y][1])
        arrived.append(block if at == 0 else swap(block, x=x, y=y))
    return arrived


def from_chips(place, blocks):
    arrived = [
        blocks[at] if at == 0 else swap(blocks[at], x=x, y=y) for at, (x, y) in enumerate(CHIPS)
    ]
    ordered = []
    for y in range(2):
        near, far = arrived[y], arrived[2 + y]
        ordered.append(jnp.where(place.x == 0, near, far))
        ordered.append(jnp.where(place.x == 0, far, near))
    return (ordered, arrived[1:])


def block_forward(place, resid, modulation, weights, biases, size, hook):
    (attn, up, down) = weights
    (query_bias, value_bias, proj_bias, up_bias, down_bias) = biases
    latents, tokens, width = resid.shape
    (shift_one, scale_one, gate_one, shift_two, scale_two, gate_two) = modulation
    normed_one, scaling_one = normalize(resid)
    entry_one = (normed_one * (1.0 + scale_one) + shift_one).astype(LOW).reshape(-1, width)
    (near, far) = attn.both()
    four = unrelate([near[:, :width], far[:, :width], near[:, width:], far[:, width:]], place.ctx)
    qkv_weight = jnp.concatenate(four[:3], axis=1)
    proj_weight = four[3]
    projected = dot(entry_one, qkv_weight)
    queries = (projected[:, :width] + query_bias).astype(LOW)
    keys = projected[:, width : 2 * width].astype(LOW)
    values = (projected[:, 2 * width :] + value_bias).astype(LOW)
    part = width // 4

    def block(at):
        members = [member[:, at * part : (at + 1) * part] for member in (keys, values, queries)]
        return jnp.concatenate(members, axis=1)

    own = to_chips(place, [[block(0), block(1)], [block(2), block(3)]])
    other = [swap(member, core=1) for member in own]
    hook("qkv", own[1:])
    own = [member.reshape(latents, tokens, -1) for member in own]
    other = [member.reshape(latents, tokens, -1) for member in other]
    attn_out, logsum = attend(own, other, size)
    pieces, arrived = from_chips(place, [member.reshape(-1, part) for member in attn_out])
    hook("out", arrived)
    context = jnp.concatenate(pieces, axis=1)
    attended = (dot_nt(context, proj_weight) + proj_bias).reshape(resid.shape)
    middle = resid + gate_one * attended
    normed_two, scaling_two = normalize(middle)
    entry_two = (normed_two * (1.0 + scale_two) + shift_two).astype(LOW).reshape(-1, width)
    up_pair, down_pair = up.both(), down.both()
    hidden_pre = [dot(entry_two, up_pair[at]) + up_bias[at] for at in range(2)]
    hidden = [activation(member).astype(LOW) for member in hidden_pre]
    mlp_out = dot_nt(hidden[0], down_pair[0]) + dot_nt(hidden[1], down_pair[1])
    mlp_out = (mlp_out + down_bias).reshape(resid.shape)
    result = middle + gate_two * mlp_out
    saved = (
        normed_one,
        scaling_one,
        entry_one,
        own,
        other,
        logsum,
        context,
        attended,
        normed_two,
        scaling_two,
        entry_two,
        hidden_pre,
        hidden,
        mlp_out,
        qkv_weight,
        proj_weight,
    )
    return (result, saved)


def block_backward(place, upstream, modulation, weights, saved, size, earlier):
    (attn, up, down) = weights
    (
        normed_one,
        scaling_one,
        entry_one,
        own,
        other,
        logsum,
        context,
        attended,
        normed_two,
        scaling_two,
        entry_two,
        hidden_pre,
        hidden,
        mlp_out,
        qkv_weight,
        proj_weight,
    ) = saved
    up_pair, down_pair = up.both(), down.both()
    latents, tokens, width = upstream.shape
    part = width // 4
    unit_width = width // 2
    (shift_one, scale_one, gate_one, shift_two, scale_two, gate_two) = modulation
    gate_two_grad = jnp.sum(upstream * mlp_out, axis=1)
    mlp_grad = (gate_two * upstream).astype(LOW).reshape(-1, width)
    down_bias_grad = jnp.sum(mlp_grad, axis=0, keepdims=True, dtype=FULL)
    down_grad = Grad(
        lambda lo, hi: dot_tn(mlp_grad, hidden[0][:, lo:hi]),
        dot_tn(mlp_grad, hidden[1]),
        unit_width,
        True,
    )
    pre_grad = []
    for at in (1, 0):
        unused_value, gelu_pull = jax.vjp(activation, hidden_pre[at])
        pre_grad.insert(0, gelu_pull(dot(mlp_grad, down_pair[at]))[0].astype(LOW))
    up_bias_grad = jnp.stack([jnp.sum(member, axis=0, dtype=FULL) for member in pre_grad])
    up_grad = Grad(
        lambda lo, hi: dot_tn(entry_two, pre_grad[0][:, lo:hi]),
        dot_tn(entry_two, pre_grad[1]),
        unit_width,
        False,
    )
    entry_two_grad = dot_nt(pre_grad[0], up_pair[0]) + dot_nt(pre_grad[1], up_pair[1])
    entry_two_grad = entry_two_grad.reshape(upstream.shape)
    scale_two_grad = jnp.sum(entry_two_grad * normed_two, axis=1)
    shift_two_grad = jnp.sum(entry_two_grad, axis=1)
    middle_grad = upstream + norm_back(entry_two_grad * (1.0 + scale_two), normed_two, scaling_two)
    gate_one_grad = jnp.sum(middle_grad * attended, axis=1)
    attended_grad = (gate_one * middle_grad).astype(LOW).reshape(-1, width)
    proj_bias_grad = jnp.sum(attended_grad, axis=0, keepdims=True, dtype=FULL)
    context_grad = dot(attended_grad, proj_weight).astype(LOW)
    blocks = [
        [context_grad[:, (2 * rel + at) * part : (2 * rel + at + 1) * part] for at in range(2)]
        for rel in range(2)
    ]
    if earlier is not None:
        blocks = tie(blocks, [earlier[0].side, earlier[1].cross, earlier[2].cross])
    out_grad = to_chips(place, blocks)
    ready = [down_grad.ready_first(), up_grad.ready_first()]
    down_grad.first(out_grad[1:])
    up_grad.first(out_grad[1:])
    if earlier is not None:
        ready.append(earlier[0].ready_second())
        earlier[0].second(out_grad[1:])
    out_grad = [member.reshape(latents, tokens, part) for member in out_grad]
    out_grad = tie(out_grad, ready)
    query_part, kv_own, kv_other = attend_back(own, other, out_grad, logsum, size)
    kv_part = (kv_own + swap(kv_other, core=1)).astype(LOW)
    blocks = [
        jnp.concatenate([kv_part[at], query_part[at]], axis=-1).reshape(-1, 3 * part)
        for at in range(4)
    ]
    due = [down_grad.side, up_grad.side]
    if earlier is not None:
        due.append(earlier[0].cross)
    pieces, arrived = from_chips(place, tie(blocks, due))
    ready = [down_grad.ready_second(), up_grad.ready_second()]
    down_grad.second(arrived)
    up_grad.second(arrived)
    pieces = tie(pieces, ready)
    triple = [
        jnp.concatenate([member[:, at * part : (at + 1) * part] for member in pieces], axis=1)
        for at in (2, 0, 1)
    ]
    query_bias_grad = jnp.sum(triple[0], axis=0, keepdims=True, dtype=FULL)
    value_bias_grad = jnp.sum(triple[2], axis=0, keepdims=True, dtype=FULL)
    entry_one_grad = dot_nt(jnp.concatenate(triple, axis=1), qkv_weight).reshape(upstream.shape)
    scale_one_grad = jnp.sum(entry_one_grad * normed_one, axis=1)
    shift_one_grad = jnp.sum(entry_one_grad, axis=1)
    resid_grad = middle_grad + norm_back(
        entry_one_grad * (1.0 + scale_one), normed_one, scaling_one
    )
    rights = jnp.stack([*triple, context])

    def attn_term(at, lo, hi):
        matrix = place.ctx ^ at
        left = jnp.where(matrix == 3, attended_grad, entry_one)
        right = lax.dynamic_index_in_dim(rights, matrix, 0, keepdims=False)
        return dot_tn(left, right[:, lo:hi])

    attn_grad = Grad(
        lambda lo, hi: attn_term(2, lo - width, hi - width) if lo >= width else attn_term(0, lo, hi),
        jnp.concatenate(
            [attn_term(1, 0, width).astype(LOW), attn_term(3, 0, width).astype(LOW)], axis=1
        ),
        unit_width,
        False,
    )
    attn_grad.ready_first()
    attn_grad.first()

    def halves(row):
        return jnp.concatenate(place.by_y(row[:, : width // 2], row[:, width // 2 :]), axis=1)

    up_rows = jnp.dot(
        place.unit_matrix(), up_bias_grad.reshape(8, unit_width), precision=PRECISE
    ).reshape(4, width)
    def placed(value, at):
        return jnp.pad(value, ((at, 8 - at - value.shape[0]), (0, 0)))

    biases = [halves(query_bias_grad), halves(value_bias_grad), proj_bias_grad, down_bias_grad]
    biases = sum(placed(member, at) for at, member in enumerate(biases)) + placed(up_rows, 4)
    spans = [
        shift_one_grad,
        scale_one_grad,
        gate_one_grad,
        shift_two_grad,
        scale_two_grad,
        gate_two_grad,
    ]
    small = jnp.concatenate([*[placed(member, 0) for member in spans], biases], axis=0)
    return (resid_grad, (attn_grad, up_grad, down_grad), small)


def local(
    mesh,
    latents_in,
    condition,
    out_grad,
    mod_weight,
    mod_bias,
    qkv_weight,
    qkv_bias,
    proj_weight,
    proj_bias,
    fc1_weight,
    fc1_bias,
    fc2_weight,
    fc2_bias,
):
    place = Place(mesh)
    n_dp = place.n_dp
    layers = mod_weight.shape[0]
    latents, ctx_tokens, width = latents_in.shape
    tokens = ctx_tokens // 2
    rows = width // n_dp
    heads = qkv_bias.shape[2]
    size = qkv_bias.shape[3] * n_dp
    quarter = fc1_weight.shape[2] // 4
    spans = mod_bias.shape[1]

    start = place.ctx * quarter
    quarters = []
    for layer in range(layers):
        attn = pick(place.ctx, [*[qkv_weight[layer, at] for at in range(3)], proj_weight[layer]])
        mlp = [
            lax.dynamic_slice_in_dim(member[layer], start, quarter, 1)
            for member in (fc1_weight, fc2_weight)
        ]
        quarters.append([attn, *mlp])
    attn = place.gather_dp(quarters[0][0]).reshape(width, quarter)
    after = lax.all_gather(jnp.stack(quarters[0][1:]), "dp", axis=1, tiled=True)
    packs = [[attn, after[0], after[1]]]
    for layer in range(1, layers):
        whole = tie(jnp.stack(quarters[layer]), after)
        after = lax.all_gather(whole, "dp", axis=1, tiled=True)
        packs.append([after[0], after[1], after[2]])
    weights = [
        (Weight(pack[0], False), Weight(pack[1], False), Weight(pack[2], True)) for pack in packs
    ]
    weights[0][0].first()
    weights[0][0].second()
    weights[0][1].first()
    weights[0][2].first(weights[0][0].cross)

    members = (mod_bias, qkv_bias, proj_bias, fc1_bias, fc2_bias)
    flat = jnp.concatenate(
        [condition.reshape(-1)] + [member.astype(FULL).reshape(-1) for member in members]
    )
    mine = place.gather_dp(flat)
    cond_all = mine[:, : condition.size].reshape(n_dp * latents, width)
    silu_all = jax.nn.silu(cond_all)
    silu_rows = lax.dynamic_slice_in_dim(silu_all, place.z * rows, rows, 1)
    mine = mine[:, condition.size :]
    pair = place.by_y(mine, swap(mine, y=1))
    everyone = jnp.stack(pair, axis=1)
    taken = []
    offset = 0
    for member in members:
        source = everyone if member.ndim > 2 and member is not mod_bias else mine
        part = lax.slice_in_dim(source, offset, offset + member.size, axis=-1)
        taken.append(part.reshape(source.shape[:-1] + member.shape))
        offset += member.size
    mod_bias_half = jnp.moveaxis(taken[0], 0, 2).reshape(layers, 1, spans * width)
    qkv_all = jnp.transpose(taken[1], (1, 2, 3, 4, 0, 5)).reshape(2, layers, 2, heads * size)
    qkv_bias_all = jnp.where(place.y == 0, qkv_all, qkv_all[::-1])
    proj_bias_all = jnp.moveaxis(taken[2], 0, 1).reshape(layers, width)
    fc1_all = jnp.transpose(taken[3], (2, 1, 3, 0, 4)).reshape(layers, 8, quarter)
    fc1_rel = jnp.einsum("ar,lae->lre", place.unit_matrix(), fc1_all, precision=PRECISE)
    fc2_bias_all = jnp.moveaxis(taken[4], 0, 1).reshape(layers, width)

    halfmod = jnp.einsum(
        "bd,lde->lbe", silu_rows, mod_weight.astype(FULL), precision=PRECISE
    ).reshape(layers, n_dp, latents, -1)
    halfmod = place.scatter_dp(
        lambda at: lax.dynamic_index_in_dim(halfmod, at, 1, keepdims=False), FULL
    )
    halfmod = halfmod + mod_bias_half
    by_half = place.by_y(halfmod, swap(halfmod, y=1))
    modulations = [
        [
            by_half[at // spans][layer, :, None, at % spans * width : (at % spans + 1) * width]
            for at in range(2 * spans)
        ]
        for layer in range(layers)
    ]

    token_start = place.y * tokens
    resid = lax.dynamic_slice_in_dim(latents_in, token_start, tokens, 1).astype(FULL)
    upstream = lax.dynamic_slice_in_dim(out_grad, token_start, tokens, 1).astype(FULL)
    saved_list = []
    all_biases = [
        (
            qkv_bias_all[:, layer, 0].reshape(1, -1),
            qkv_bias_all[:, layer, 1].reshape(1, -1),
            proj_bias_all[layer].reshape(1, -1),
            [fc1_rel[layer, 4 * core : 4 * core + 4].reshape(1, -1) for core in range(2)],
            fc2_bias_all[layer].reshape(1, -1),
        )
        for layer in range(layers)
    ]
    resid, modulations, all_biases = lax.optimization_barrier((resid, modulations, all_biases))
    for layer in range(layers):
        biases = all_biases[layer]

        def hook(event, arrived):
            if event == "qkv":
                for member in weights[layer][1:]:
                    member.second(arrived)
                if layer + 1 < layers:
                    weights[layer + 1][0].first(arrived)
                    weights[layer + 1][0].second()
            elif layer + 1 < layers:
                for member in weights[layer + 1][1:]:
                    member.first(arrived)

        resid, saved = block_forward(
            place, resid, modulations[layer], weights[layer], biases, size, hook
        )
        saved_list.append(saved)

    def both_halves(value):
        return jnp.concatenate(place.by_y(value, swap(value, y=1)), axis=1)

    block_out = both_halves(resid.astype(LOW))

    def scatter_units(members):
        units = jnp.concatenate([member.unit().astype(LOW) for member in members], axis=1)
        return lax.psum_scatter(units, "dp", scatter_dimension=0, tiled=True)

    shards = [None] * layers
    smalls = [None] * layers
    earlier = None
    for layer in reversed(range(layers)):
        upstream, grads, smalls[layer] = block_backward(
            place, upstream, modulations[layer], weights[layer], saved_list[layer], size, earlier
        )
        if earlier is not None:
            shards[layer + 1] = scatter_units(earlier)
        earlier = grads
    latents_grad = both_halves(upstream)
    (attn_grad, up_grad, down_grad) = earlier
    both = scatter_units([up_grad, down_grad])
    attn_grad.ready_second()
    attn_grad.second()
    attn = attn_grad.unit()
    attn = place.scatter_dp(
        lambda at: lax.dynamic_slice_in_dim(attn, at * rows, rows, 0), LOW
    ).astype(LOW)

    small = jnp.stack(smalls)
    small = small + swap(small, core=1)
    small = small + swap(small, y=1)
    small = place.gather_dp(small + swap(small, x=1))
    own_mod = lax.dynamic_slice_in_dim(small, place.y * 8 * spans, 8 * spans, 2)
    own_mod = own_mod.reshape(n_dp, layers, spans, 8, width)[:, :, :, :latents]
    own_mod = jnp.transpose(own_mod, (1, 0, 3, 2, 4)).reshape(layers, n_dp * latents, -1)
    mod_wgrad = jnp.einsum("bd,lbe->lde", silu_rows, own_mod, precision=PRECISE)
    mod_bsum = jnp.sum(own_mod, axis=1).reshape(layers, spans, width)
    mod_bgrad = lax.dynamic_slice_in_dim(mod_bsum, place.z * rows, rows, 2)
    cond_part = jnp.einsum("lbe,lde->bd", own_mod, mod_weight.astype(FULL), precision=PRECISE)
    bias_sum = jnp.sum(small[:, :, 16 * spans :], axis=0)
    cond_part = cond_part + swap(cond_part, y=1)
    cond_blocks = place.gather_dp(cond_part).reshape(n_dp, n_dp, latents, rows)
    cond_sum = lax.dynamic_index_in_dim(cond_blocks, place.z, 1, keepdims=False)
    cond_sum = jnp.moveaxis(cond_sum, 0, 1).reshape(latents, width)
    unused_value, silu_pull = jax.vjp(jax.nn.silu, condition)
    condition_grad = silu_pull(cond_sum)[0]

    qkv_b = bias_sum[:, :2].reshape(layers, 2, 2, heads, n_dp, -1)
    qkv_b = lax.dynamic_index_in_dim(qkv_b, place.y, 2, keepdims=False)
    qkv_bgrad = lax.dynamic_index_in_dim(qkv_b, place.z, 3, keepdims=False)
    out_b = lax.dynamic_slice_in_dim(bias_sum[:, 2:4], place.z * rows, rows, 2)
    fc1_b = bias_sum[:, 4:].reshape((layers, 2, fc1_bias.shape[1], n_dp, -1))
    fc1_b = lax.dynamic_index_in_dim(fc1_b, place.y, 1, keepdims=False)
    fc1_bgrad = lax.dynamic_index_in_dim(fc1_b, place.z, 2, keepdims=False)

    qkv_wgrad, proj_wgrad = [None] * layers, [None] * layers
    fc1_wgrad, fc2_wgrad = [None] * layers, [None] * layers
    for layer in range(layers):
        if layer > 0:
            units = spread_ctx(place, shards[layer])
            attn_units = [member[:, :quarter] for member in units]
            both_units = [member[:, quarter:] for member in units]
        else:
            both_units = spread_ctx(place, both)
            attn_units = spread_ctx(place, attn)
        qkv_wgrad[layer] = jnp.stack(attn_units[:3]).astype(FULL)
        proj_wgrad[layer] = attn_units[3].astype(FULL)
        fc1_wgrad[layer] = jnp.concatenate([member[:, :quarter] for member in both_units], axis=1)
        fc2_wgrad[layer] = jnp.concatenate([member[:, quarter:] for member in both_units], axis=1)
    return (
        block_out,
        latents_grad,
        condition_grad,
        mod_wgrad,
        mod_bgrad,
        jnp.stack(qkv_wgrad),
        qkv_bgrad,
        jnp.stack(proj_wgrad),
        out_b[:, 0],
        jnp.stack(fc1_wgrad).astype(FULL),
        fc1_bgrad,
        jnp.stack(fc2_wgrad).astype(FULL),
        out_b[:, 1],
    )


def solution(mesh):
    placed = (
        P("dp", "ctx", None),
        P("dp", None),
        P("dp", "ctx", None),
        P(None, "dp", "tp"),
        P(None, "tp", "dp"),
        P(None, None, "dp", "tp"),
        P(None, None, "tp", "dp"),
        P(None, "dp", "tp"),
        P(None, "dp"),
        P(None, "dp", "tp"),
        P(None, "tp", "dp"),
        P(None, "dp", "tp"),
        P(None, "dp"),
    )
    outs = (
        P("dp", "ctx", None),
        P("dp", "ctx", None),
        P("dp", None),
        P(None, "dp", "tp"),
        P(None, "tp", "dp"),
        P(None, None, "dp", "tp"),
        P(None, None, "tp", "dp"),
        P(None, "dp", "tp"),
        P(None, "dp"),
        P(None, "dp", "tp"),
        P(None, "tp", "dp"),
        P(None, "dp", "tp"),
        P(None, "dp"),
    )
    return jax.shard_map(
        lambda *arrays: local(mesh, *arrays),
        mesh=mesh,
        in_specs=placed,
        out_specs=outs,
        check_vma=False,
    )
```

time: 1050 us -> 940 us (0.90)
  starting transfers between devices: 148 us -> 96.6 us
  local copies, waits for them, and re-layouts: 172 us -> 130 us
  other arithmetic: 170 us -> 145 us
  matrix products: 95.1 us -> 115 us
  waiting for transfers between devices: 381 us -> 362 us
  between operations: 4.92 us -> 18 us
    ppermute x48 -> x18, starting transfers between devices: 72.8 us -> 31.7 us  [swap_dp(): return lax.ppermute(value, 'dp', [(at, at ^ mask) for at in range(count)])]
    another operation x22 -> x8, local copies, waits for them, and re-layouts: 19.7 us -> 2.14 us  [the longest x1 1.33 us: spread_ctx(): far = swap(jnp.stack([unit, over_x]), core=1)]
    dot_general x16 -> x28, matrix products: 37.8 us -> 54.9 us  [dot_tn(): lax.dot_general(left, right, (((0,), (0,)), ((), ())), preferred_element_...]
    ppermute x48 -> x18, waiting for transfers between devices: 59.4 us -> 43 us  [swap_dp(): return lax.ppermute(value, 'dp', [(at, at ^ mask) for at in range(count)])]
    add x24 -> x9, other arithmetic: 23.4 us -> 7.55 us  [the longest x1 1.73 us: local(): small = small + swap(small, y=1)]
    optimization_barrier x0 -> x12, other arithmetic: none -> 14.8 us  [local(): lax.optimization_barrier((resid, modulations, all_biases))]
    another operation x16 -> x11, other arithmetic: 18.6 us -> 4.69 us  [the longest x2 1.23 us: block_backward(): jnp.stack([jnp.sum(member, axis=0, dtype=FULL) for member in pre_grad])]
    add x11 -> x1, local copies, waits for them, and re-layouts: 13.9 us -> 0.69 us  [local(): halfmod = halfmod + mod_bias_half]
  transfers between devices with their start and end apart: 132 -> 106, of which waited for: 52 -> 40; matrix products, arithmetic and copies ran while one was open for 36% -> 33% of each run, Pallas kernels for 6% -> 3%
where the time goes in v2:
time: 940 us; the launch traced here: 929 us
  waiting for transfers between devices  362 us (39%)
  other arithmetic  145 us (15%)
  local copies, waits for them, and re-layouts  130 us (14%)
  matrix products  115 us (12%)
  starting transfers between devices  96.6 us (10%)
  Pallas kernels  62.1 us (7%)
  between operations  18 us (2%)
    ppermute x84, waiting for transfers between devices, swap(): return lax.ppermute(value, PLANE, [(at, at ^ mask) for at in range(8)])  315 us
    ppermute x84, starting transfers between devices, swap(): return lax.ppermute(value, PLANE, [(at, at ^ mask) for at in range(8)])  64.4 us
    unnamed x594, local copies, waits for them, and re-layouts  58.7 us
    dot_general x28, matrix products, dot_tn(): lax.dot_general(left, right, (((0,), (0,)), ((), ())), preferred_element_...  54.9 us
    ppermute x18, waiting for transfers between devices, swap_dp(): return lax.ppermute(value, 'dp', [(at, at ^ mask) for at in range(count)])  43 us
    pallas_call x2, Pallas kernels, attend_back(): pl.pallas_call(lambda *refs: attend_back_kernel(size, size ** (-0.5), *re...  37.8 us
    ppermute x18, starting transfers between devices, swap_dp(): return lax.ppermute(value, 'dp', [(at, at ^ mask) for at in range(count)])  31.7 us
    dot_general x12, matrix products, dot(): return jnp.dot(left, right, preferred_element_type=FULL)  24.9 us
  transfers between devices with their start and end apart: 106, of which 40 were waited for; matrix products, arithmetic and copies ran while one was open for 33% of the time, Pallas kernels for 3%

profile of v2, /device:TPU:0, one launch (start us, length us, event | category | flops | bytes accessed | tf_op | source)
XLA Modules:
  0.0 929.3 jit_solution(5742828108650448542)
XLA Ops:
  81.4 17.7 %collective-permute-done.12 = bf16[768,768]{1,0:T(8,128)(2,1)} collective-permute-done((bf16[768,768]{1,0:T(8,128)(2,1)}, bf16[768,768]{1,0:T(8,128)(2,1)}, u32[]{:S(2)}, u32[]{:S(2)}) %collective-permute-start.12) | collective-permute-done | bytes 1179680 | tf_op jit(solution)/shard_map/ppermute | solution.py:19
  133.6 17.7 %collective-permute-done.14 = bf16[384,576]{1,0:T(8,128)(2,1)} collective-permute-done((bf16[384,576]{1,0:T(8,128)(2,1)S(1)}, bf16[384,576]{1,0:T(8,128)(2,1)}, u32[]{:S(2)}, u32[]{:S(2)}) %collective-permute-start.14) | collective-permute-done | bytes 442400 | tf_op jit(solution)/shard_map/ppermute | solution.py:19
  169.1 12.4 %attention_forward.2 = (bf16[3,128,192]{2,1,0:T(8,128)(2,1)}, bf16[3,128,192]{2,1,0:T(8,128)(2,1)}, bf16[3,128,192]{2,1,0:T(8,128)(2,1)}, bf16[3,128,192]{2,1,0:T(8,128)(2,1)}, f32[3,512,3]{2,1,0:T(8,128)}) custom-call(bf16[3,128,576]{2,1,0:T(8,128)(2,1)} %maximum_select_fusion.refs_0_, bf16[3,128,576]{2,1,0:T(8,128)(2,1)} %bitcast.46.refs_1_, ...), custom_call_target="tpu_custom_call" | custom-call | flops 1207959552 | bytes 4128768 | tf_op jit(solution)/shard_map/attention_forward/pallas_call | solution.py:147
  202.5 9.1 collective-permute-done.22
  226.5 10.9 %collective-permute-done.31 = bf16[768,768]{1,0:T(8,128)(2,1)S(1)} collective-permute-done((bf16[768,768]{1,0:T(8,128)(2,1)S(1)}, bf16[768,768]{1,0:T(8,128)(2,1)S(1)}, u32[]{:S(2)}, u32[]{:S(2)}) %collective-permute-start.31) | collective-permute-done | bytes 1179680 | tf_op jit(solution)/shard_map/ppermute | solution.py:19
  258.5 8.8 collective-permute-done.33
  269.1 10.9 %collective-permute-done.35 = bf16[384,576]{1,0:T(8,128)(2,1)} collective-permute-done((bf16[384,576]{1,0:T(8,128)(2,1)S(1)}, bf16[384,576]{1,0:T(8,128)(2,1)}, u32[]{:S(2)}, u32[]{:S(2)}) %collective-permute-start.35) | collective-permute-done | bytes 442400 | tf_op jit(solution)/shard_map/ppermute | solution.py:19
  293.5 12.0 %attention_forward.3 = (bf16[3,128,192]{2,1,0:T(8,128)(2,1)}, bf16[3,128,192]{2,1,0:T(8,128)(2,1)}, bf16[3,128,192]{2,1,0:T(8,128)(2,1)}, bf16[3,128,192]{2,1,0:T(8,128)(2,1)}, f32[3,512,3]{2,1,0:T(8,128)}) custom-call(bf16[3,128,576]{2,1,0:T(8,128)(2,1)} %maximum_select_fusion.1.refs_0_, bf16[3,128,576]{2,1,0:T(8,128)(2,1)} %bitcast.72.refs_1_, ...), custom_call_target="tpu_custom_call" | custom-call | flops 1207959552 | bytes 4128768 | tf_op jit(solution)/shard_map/attention_forward/pallas_call | solution.py:147
  317.7 25.8 %collective-permute-done.40 = bf16[384,192]{1,0:T(8,128)(2,1)S(1)} collective-permute-done((bf16[384,192]{1,0:T(8,128)(2,1)S(1)}, bf16[384,192]{1,0:T(8,128)(2,1)S(1)}, u32[]{:S(2)}, u32[]{:S(2)}) %collective-permute-start.40) | collective-permute-done | bytes 147488 | tf_op jit(solution)/shard_map/ppermute | solution.py:19
  386.7 18.7 %attention_backward.2 = (bf16[4,3,128,192]{3,2,1,0:T(8,128)(2,1)}, f32[4,3,128,384]{3,2,1,0:T(8,128)}, f32[4,3,128,384]{3,2,1,0:T(8,128)}) custom-call(bf16[3,128,576]{2,1,0:T(8,128)(2,1)} %maximum_select_fusion.1.refs_0_, bf16[3,128,576]{2,1,0:T(8,128)(2,1)} %bitcast.72.refs_1_, bf16[3,128,576]{2,1,0:T(8,128)(2,1)} %bitcast.73.refs_2_, ...), custom_call_target="tpu_custom_call" | custom-call | flops 3019898880 | bytes 9437184 | tf_op jit(solution)/shard_map/attention_backward/pallas_call | solution.py:217
  433.4 23.1 %collective-permute-done.56 = bf16[768,768]{0,1:T(8,128)(2,1)S(1)} collective-permute-done((bf16[768,768]{0,1:T(8,128)(2,1)S(1)}, bf16[768,768]{0,1:T(8,128)(2,1)S(1)}, u32[]{:S(2)}, u32[]{:S(2)}) %collective-permute-start.56) | collective-permute-done | bytes 1179680 | tf_op jit(solution)/shard_map/ppermute | solution.py:19
  471.1 8.9 collective-permute-done.60
  553.4 17.8 %collective-permute-done.62 = bf16[768,768]{0,1:T(8,128)(2,1)S(1)} collective-permute-done((bf16[768,768]{0,1:T(8,128)(2,1)S(1)}, bf16[768,768]{0,1:T(8,128)(2,1)S(1)}, u32[]{:S(2)}, u32[]{:S(2)}) %collective-permute-start.62) | collective-permute-done | bytes 1179680 | tf_op jit(solution)/shard_map/ppermute | solution.py:19
  584.0 19.1 %attention_backward.3 = (bf16[4,3,128,192]{3,2,1,0:T(8,128)(2,1)}, f32[4,3,128,384]{3,2,1,0:T(8,128)}, f32[4,3,128,384]{3,2,1,0:T(8,128)}) custom-call(bf16[3,128,576]{2,1,0:T(8,128)(2,1)} %maximum_select_fusion.refs_0_, bf16[3,128,576]{2,1,0:T(8,128)(2,1)} %bitcast.46.refs_1_, bf16[3,128,576]{2,1,0:T(8,128)(2,1)} %bitcast.47.refs_2_, ...), custom_call_target="tpu_custom_call" | custom-call | flops 3019898880 | bytes 9437184 | tf_op jit(solution)/shard_map/attention_backward/pallas_call | solution.py:217
  623.0 7.9 collective-permute-done.73
  642.7 13.1 %collective-permute-done.71 = bf16[768,768]{0,1:T(8,128)(2,1)} collective-permute-done((bf16[768,768]{0,1:T(8,128)(2,1)}, bf16[768,768]{0,1:T(8,128)(2,1)}, u32[]{:S(2)}, u32[]{:S(2)}) %collective-permute-start.71) | collective-permute-done | bytes 1179680 | tf_op jit(solution)/shard_map/ppermute | solution.py:19
  670.1 10.1 %collective-permute-done.76 = bf16[384,576]{1,0:T(8,128)(2,1)S(1)} collective-permute-done((bf16[384,576]{1,0:T(8,128)(2,1)S(1)}, bf16[384,576]{1,0:T(8,128)(2,1)S(1)}, u32[]{:S(2)}, u32[]{:S(2)}) %collective-permute-start.76) | collective-permute-done | bytes 442400 | tf_op jit(solution)/shard_map/ppermute | solution.py:19
  716.1 8.2 collective-permute-done.99
  725.9 21.5 %collective-permute-done.79 = f32[2,56,768]{2,1,0:T(8,128)S(1)} collective-permute-done((f32[2,56,768]{2,1,0:T(8,128)S(1)}, f32[2,56,768]{2,1,0:T(8,128)S(1)}, u32[]{:S(2)}, u32[]{:S(2)}) %collective-permute-start.79) | collective-permute-done | bytes 344096 | tf_op jit(solution)/shard_map/ppermute | solution.py:19
  768.5 17.7 %collective-permute-done.81 = f32[2,56,768]{2,1,0:T(8,128)S(1)} collective-permute-done((f32[2,56,768]{2,1,0:T(8,128)S(1)}, f32[2,56,768]{2,1,0:T(8,128)S(1)}, u32[]{:S(2)}, u32[]{:S(2)}) %collective-permute-start.81) | collective-permute-done | bytes 344096 | tf_op jit(solution)/shard_map/ppermute | solution.py:23
  786.1 14.9 %collective-permute-done.82 = f32[2,56,768]{2,1,0:T(8,128)S(1)} collective-permute-done((f32[2,56,768]{2,1,0:T(8,128)S(1)}, f32[2,56,768]{2,1,0:T(8,128)S(1)}, u32[]{:S(2)}, u32[]{:S(2)}) %collective-permute-start.82) | collective-permute-done | bytes 344096 | tf_op jit(solution)/shard_map/ppermute | solution.py:23
  846.4 29.6 %collective-permute-done.100 = bf16[192,768]{1,0:T(8,128)(2,1)S(1)} collective-permute-done((bf16[192,768]{1,0:T(8,128)(2,1)}, bf16[192,768]{1,0:T(8,128)(2,1)S(1)}, u32[]{:S(2)}, u32[]{:S(2)}) %collective-permute-start.100) | collective-permute-done | bytes 294944 | tf_op jit(solution)/shard_map/ppermute | solution.py:19
  881.2 13.9 %collective-permute-done.90 = bf16[768,384]{1,0:T(8,128)(2,1)S(1)} collective-permute-done((bf16[768,384]{1,0:T(8,128)(2,1)S(1)}, bf16[768,384]{1,0:T(8,128)(2,1)S(1)}, u32[]{:S(2)}, u32[]{:S(2)}) %collective-permute-start.90) | collective-permute-done | bytes 589856 | tf_op jit(solution)/shard_map/ppermute | solution.py:19
  905.4 7.7 collective-permute-done.92
  (1152 shorter events, 553.8 us)
Async XLA Ops:
  7.2 104.6 %all-gather.3.cloned.1.call-start = ((), (), s32[]{:S(2)}) async-start(), calls=%async_computation.2 | async-start | bytes 1474560 | tf_op jit(solution)/shard_map/all_gather | solution.py:557
  36.7 119.5 %all-gather.5.cloned.1.call-start = ((), (), s32[]{:S(2)}) async-start(), calls=%async_computation.3 | async-start | bytes 2211840 | tf_op jit(solution)/shard_map/all_gather | solution.py:561
  114.9 650.8 %reduce-scatter.7.cloned.1.call-start = ((), (), s32[]{:S(2)}) async-start(), calls=%async_computation.4 | async-start | bytes 2211840 | tf_op jit(solution)/shard_map/reduce_scatter | solution.py:654
  127.8 34.3 %collective-permute-start.26 = (bf16[768,384]{1,0:T(8,128)(2,1)}, bf16[768,384]{1,0:T(8,128)(2,1)}, u32[]{:S(2)}, u32[]{:S(2)}) collective-permute-start(bf16[768,384]{1,0:T(8,128)(2,1)} %get-tuple-element.116), channel_id=1, source_target_pairs={{0,4},{1,5},{2,6},{3,7},{4,0},{5,1},{6,2},{7,3},{8,12},{9,13},{10,... | collective-permute-start | bytes 1769480 | tf_op jit(solution)/shard_map/ppermute | solution.py:19
  130.6 32.9 %collective-permute-start.17 = (bf16[384,576]{1,0:T(8,128)(2,1)}, bf16[384,576]{1,0:T(8,128)(2,1)}, u32[]{:S(2)}, u32[]{:S(2)}) collective-permute-start(bf16[384,576]{1,0:T(8,128)(2,1)} %get-tuple-element.357), channel_id=1, source_target_pairs={{0,2},{1,3},{2,0},{3,1},{4,6},{5,7},{6,4},{7,5},{8,10},{9,11},{10,... | collective-permute-start | bytes 1327112 | tf_op jit(solution)/shard_map/ppermute | solution.py:19
  162.1 51.3 %collective-permute-start.25 = (bf16[768,768]{1,0:T(8,128)(2,1)}, bf16[768,768]{1,0:T(8,128)(2,1)}, u32[]{:S(2)}, u32[]{:S(2)}) collective-permute-start(bf16[768,768]{1,0:T(8,128)(2,1)} %pad_maximum_fusion.20), channel_id=1, source_target_pairs={{0,4},{1,5},{2,6},{3,7},{4,0},{5,1},{6,2},{7,3},{8,12},{9,13},{10,... | collective-permute-start | bytes 3538952 | tf_op jit(solution)/shard_map/ppermute | solution.py:19
  163.5 36.1 %collective-permute-start.30 = (bf16[768,384]{1,0:T(8,128)(2,1)}, bf16[768,384]{1,0:T(8,128)(2,1)}, u32[]{:S(2)}, u32[]{:S(2)}) collective-permute-start(bf16[768,384]{1,0:T(8,128)(2,1)} %get-tuple-element.124), channel_id=1, source_target_pairs={{0,1},{1,0},{2,3},{3,2},{4,5},{5,4},{6,7},{7,6},{8,9},{9,8},{10,11... | collective-permute-start | bytes 1769480 | tf_op jit(solution)/shard_map/ppermute | solution.py:19
  167.5 47.8 %collective-permute-start.27 = (bf16[768,768]{1,0:T(8,128)(2,1)}, bf16[768,768]{1,0:T(8,128)(2,1)}, u32[]{:S(2)}, u32[]{:S(2)}) collective-permute-start(bf16[768,768]{1,0:T(8,128)(2,1)} %pad_maximum_fusion.21), channel_id=1, source_target_pairs={{0,1},{1,0},{2,3},{3,2},{4,5},{5,4},{6,7},{7,6},{8,9},{9,8},{10,11... | collective-permute-start | bytes 3538952 | tf_op jit(solution)/shard_map/ppermute | solution.py:19
  258.0 50.5 %collective-permute-start.43 = (bf16[768,384]{1,0:T(8,128)(2,1)S(1)}, bf16[768,384]{1,0:T(8,128)(2,1)}, u32[]{:S(2)}, u32[]{:S(2)}) collective-permute-start(bf16[768,384]{1,0:T(8,128)(2,1)S(1)} %get-tuple-element.135), channel_id=1, source_target_pairs={{0,1},{1,0},{2,3},{3,2},{4,5},{5,4},{6,7},{7,6},{8,9},{9,8},{10,11... | collective-permute-start | bytes 1769480 | tf_op jit(solution)/shard_map/ppermute | solution.py:19
  309.6 35.8 %collective-permute-start.44 = (bf16[768,768]{1,0:T(8,128)(2,1)S(1)}, bf16[768,768]{1,0:T(8,128)(2,1)S(1)}, u32[]{:S(2)}, u32[]{:S(2)}) collective-permute-start(bf16[768,768]{1,0:T(8,128)(2,1)S(1)} %pad_maximum_fusion.23), channel_id=1, source_target_pairs={{0,4},{1,5},{2,6},{3,7},{4,0},{5,1},{6,2},{7,3},{8,12},{9,13},{10,... | collective-permute-start | bytes 3538952 | tf_op jit(solution)/shard_map/ppermute | solution.py:19
  310.4 36.4 %collective-permute-start.46 = (bf16[768,768]{1,0:T(8,128)(2,1)S(1)}, bf16[768,768]{1,0:T(8,128)(2,1)S(1)}, u32[]{:S(2)}, u32[]{:S(2)}) collective-permute-start(bf16[768,768]{1,0:T(8,128)(2,1)S(1)} %pad_maximum_fusion.24), channel_id=1, source_target_pairs={{0,1},{1,0},{2,3},{3,2},{4,5},{5,4},{6,7},{7,6},{8,9},{9,8},{10,11... | collective-permute-start | bytes 3538952 | tf_op jit(solution)/shard_map/ppermute | solution.py:19
  311.1 32.5 %collective-permute-start.40 = (bf16[384,192]{1,0:T(8,128)(2,1)S(1)}, bf16[384,192]{1,0:T(8,128)(2,1)S(1)}, u32[]{:S(2)}, u32[]{:S(2)}) collective-permute-start(bf16[384,192]{1,0:T(8,128)(2,1)S(1)} %bitcast.674), channel_id=1, source_target_pairs={{0,4},{1,5},{2,6},{3,7},{4,0},{5,1},{6,2},{7,3},{8,12},{9,13},{10,... | collective-permute-start | bytes 442376 | tf_op jit(solution)/shard_map/ppermute | solution.py:19
  603.1 34.9 %collective-permute-start.70 = (f32[4,3,128,384]{3,2,1,0:T(8,128)}, f32[4,3,128,384]{3,2,1,0:T(8,128)}, u32[]{:S(2)}, u32[]{:S(2)}) collective-permute-start(f32[4,3,128,384]{3,2,1,0:T(8,128)} %get-tuple-element.172), channel_id=1, source_target_pairs={{0,2},{1,3},{2,0},{3,1},{4,6},{5,7},{6,4},{7,5},{8,10},{9,11},{10,... | collective-permute-start | bytes 7077896 | tf_op jit(solution)/shard_map/ppermute | solution.py:19
  620.3 35.6 %collective-permute-start.71 = (bf16[768,768]{0,1:T(8,128)(2,1)}, bf16[768,768]{0,1:T(8,128)(2,1)}, u32[]{:S(2)}, u32[]{:S(2)}) collective-permute-start(bf16[768,768]{0,1:T(8,128)(2,1)} %pad_maximum_fusion.27), channel_id=1, source_target_pairs={{0,1},{1,0},{2,3},{3,2},{4,5},{5,4},{6,7},{7,6},{8,9},{9,8},{10,11... | collective-permute-start | bytes 3538952 | tf_op jit(solution)/shard_map/ppermute | solution.py:19
  621.0 34.9 %collective-permute-start.72 = (bf16[768,768]{0,1:T(8,128)(2,1)}, bf16[768,768]{0,1:T(8,128)(2,1)}, u32[]{:S(2)}, u32[]{:S(2)}) collective-permute-start(bf16[768,768]{0,1:T(8,128)(2,1)} %add_convert_fusion.2), channel_id=1, source_target_pairs={{0,4},{1,5},{2,6},{3,7},{4,0},{5,1},{6,2},{7,3},{8,12},{9,13},{10,... | collective-permute-start | bytes 3538952 | tf_op jit(solution)/shard_map/ppermute | solution.py:19
  637.8 207.6 %reduce-scatter.9.cloned.1.call-start = ((), (), s32[]{:S(2)}) async-start(), calls=%async_computation.5 | async-start | bytes 1474560 | tf_op jit(solution)/shard_map/reduce_scatter | solution.py:654
  701.1 61.2 %collective-permute-start.77 = (f32[3,128,768]{2,1,0:T(8,128)}, f32[3,128,768]{2,1,0:T(8,128)}, u32[]{:S(2)}, u32[]{:S(2)}) collective-permute-start(f32[3,128,768]{2,1,0:T(8,128)} %get-tuple-element.326), channel_id=1, source_target_pairs={{0,1},{1,0},{2,3},{3,2},{4,5},{5,4},{6,7},{7,6},{8,9},{9,8},{10,11... | collective-permute-start | bytes 3538952 | tf_op jit(solution)/shard_map/ppermute | solution.py:19
  711.4 126.3 %collective-permute-start.88 = (bf16[768,1536]{1,0:T(8,128)(2,1)}, bf16[768,1536]{1,0:T(8,128)(2,1)}, u32[]{:S(2)}, u32[]{:S(2)}) collective-permute-start(bf16[768,1536]{1,0:T(8,128)(2,1)} %pad_maximum_fusion.12), channel_id=1, source_target_pairs={{0,2},{1,3},{2,0},{3,1},{4,6},{5,7},{6,4},{7,5},{8,10},{9,11},{10,... | collective-permute-start | bytes 7077896 | tf_op jit(solution)/shard_map/ppermute | solution.py:19
  711.5 38.3 %collective-permute-start.98 = (bf16[768,384]{0,1:T(8,128)(2,1)S(1)}, bf16[768,384]{0,1:T(8,128)(2,1)S(1)}, u32[]{:S(2)}, u32[]{:S(2)}) collective-permute-start(bf16[768,384]{0,1:T(8,128)(2,1)S(1)} %copy-done.263), channel_id=1, source_target_pairs={{0,1},{1,0},{2,3},{3,2},{4,5},{5,4},{6,7},{7,6},{8,9},{9,8},{10,11... | collective-permute-start | bytes 1769480 | tf_op jit(solution)/shard_map/ppermute | solution.py:19
  713.4 34.0 %collective-permute-start.79 = (f32[2,56,768]{2,1,0:T(8,128)S(1)}, f32[2,56,768]{2,1,0:T(8,128)S(1)}, u32[]{:S(2)}, u32[]{:S(2)}) collective-permute-start(f32[2,56,768]{2,1,0:T(8,128)S(1)} %fusion.177), channel_id=1, source_target_pairs={{0,1},{1,0},{2,3},{3,2},{4,5},{5,4},{6,7},{7,6},{8,9},{9,8},{10,11... | collective-permute-start | bytes 1032200 | tf_op jit(solution)/shard_map/ppermute | solution.py:19
  757.9 43.2 %collective-permute-start.82 = (f32[2,56,768]{2,1,0:T(8,128)S(1)}, f32[2,56,768]{2,1,0:T(8,128)S(1)}, u32[]{:S(2)}, u32[]{:S(2)}) collective-permute-start(f32[2,56,768]{2,1,0:T(8,128)S(1)} %add.851), channel_id=1, source_target_pairs={{0,16},{8,24},{16,0},{24,8},{1,17},{9,25},{17,1},{25,9},{2,18},{10... | collective-permute-start | bytes 1032200 | tf_op jit(solution)/shard_map/ppermute | solution.py:23
  761.8 40.0 %collective-permute-start.83 = (f32[2,56,768]{2,1,0:T(8,128)S(1)}, f32[2,56,768]{2,1,0:T(8,128)}, u32[]{:S(2)}, u32[]{:S(2)}) collective-permute-start(f32[2,56,768]{2,1,0:T(8,128)S(1)} %add.851), channel_id=1, source_target_pairs={{0,24},{8,16},{16,8},{24,0},{1,25},{9,17},{17,9},{25,1},{2,26},{10... | collective-permute-start | bytes 1032200 | tf_op jit(solution)/shard_map/ppermute | solution.py:23
  765.7 58.8 %collective-permute-start.96 = (bf16[192,1152]{1,0:T(8,128)(2,1)}, bf16[192,1152]{1,0:T(8,128)(2,1)}, u32[]{:S(2)}, u32[]{:S(2)}) collective-permute-start(bf16[192,1152]{1,0:T(8,128)(2,1)} %reduce-scatter.7.cloned.1.call-done), channel_id=1, source_target_pairs={{0,4},{1,5},{2,6},{3,7},{4,0},{5,1},{6,2},{7,3},{8,12},{9,13},{10,... | collective-permute-start | bytes 1327112 | tf_op jit(solution)/shard_map/ppermute | solution.py:19
  841.1 36.0 %collective-permute-start.89 = (bf16[768,768]{1,0:T(8,128)(2,1)}, bf16[768,768]{1,0:T(8,128)(2,1)}, u32[]{:S(2)}, u32[]{:S(2)}) collective-permute-start(bf16[768,768]{1,0:T(8,128)(2,1)} %add_convert_fusion), channel_id=1, source_target_pairs={{0,4},{1,5},{2,6},{3,7},{4,0},{5,1},{6,2},{7,3},{8,12},{9,13},{10,... | collective-permute-start | bytes 3538952 | tf_op jit(solution)/shard_map/ppermute | solution.py:19
  (359 other events, 3163.9 us)
Sparse Core Ops, SparseCore 0:
  36.8 38.3 all-gather.2
  115.0 41.1 all-gather.4
  637.9 38.4 reduce-scatter.6
  753.3 48.0 reduce-scatter.8

commit v3 on v2

--- a/solution.py
+++ b/solution.py
@@ -439,13 +439,14 @@
         for rel in range(2)
     ]
     if earlier is not None:
-        blocks = tie(blocks, [earlier[0].side, earlier[1].cross, earlier[2].cross])
+        blocks = tie(blocks, [earlier[1].cross, earlier[2].cross])
     out_grad = to_chips(place, blocks)
     ready = [down_grad.ready_first(), up_grad.ready_first()]
     down_grad.first(out_grad[1:])
     up_grad.first(out_grad[1:])
     if earlier is not None:
         ready.append(earlier[0].ready_second())
+        ready.append(earlier[0].side)
         earlier[0].second(out_grad[1:])
     out_grad = [member.reshape(latents, tokens, part) for member in out_grad]
     out_grad = tie(out_grad, ready)
@@ -666,6 +667,7 @@
     latents_grad = both_halves(upstream)
     (attn_grad, up_grad, down_grad) = earlier
     both = scatter_units([up_grad, down_grad])
+    first_sent = attn_grad.sent
     attn_grad.ready_second()
     attn_grad.second()
     attn = attn_grad.unit()
@@ -673,10 +675,10 @@
         lambda at: lax.dynamic_slice_in_dim(attn, at * rows, rows, 0), LOW
     ).astype(LOW)
 
-    small = jnp.stack(smalls)
+    small = tie(jnp.stack(smalls), first_sent)
     small = small + swap(small, core=1)
     small = small + swap(small, y=1)
-    small = place.gather_dp(small + swap(small, x=1))
+    small = place.gather_dp(tie(small + swap(small, x=1), attn_grad.cross))
     own_mod = lax.dynamic_slice_in_dim(small, place.y * 8 * spans, 8 * spans, 2)
     own_mod = own_mod.reshape(n_dp, layers, spans, 8, width)[:, :, :, :latents]
     own_mod = jnp.transpose(own_mod, (1, 0, 3, 2, 4)).reshape(layers, n_dp * latents, -1)

time: 940 us -> 893 us (0.950)
  waiting for transfers between devices: 362 us -> 327 us
    ppermute x18, waiting for transfers between devices: 43 us -> 19.6 us  [swap_dp(): return lax.ppermute(value, 'dp', [(at, at ^ mask) for at in range(count)])]
    ppermute x84, waiting for transfers between devices: 315 us -> 295 us  [swap(): return lax.ppermute(value, PLANE, [(at, at ^ mask) for at in range(8)])]
    unnamed x594 -> x574, local copies, waits for them, and re-layouts: 58.7 us -> 52.3 us
  transfers between devices with their start and end apart: 106 -> 106, of which waited for: 40 -> 44; matrix products, arithmetic and copies ran while one was open for 33% -> 35% of each run, Pallas kernels for 3% -> 3%
where the time goes in v3:
time: 893 us; the launch traced here: 882 us
  waiting for transfers between devices  327 us (37%)
  other arithmetic  143 us (16%)
  local copies, waits for them, and re-layouts  121 us (14%)
  matrix products  115 us (13%)
  starting transfers between devices  96.5 us (11%)
  Pallas kernels  62.6 us (7%)
  between operations  17.6 us (2%)
    ppermute x84, waiting for transfers between devices, swap(): return lax.ppermute(value, PLANE, [(at, at ^ mask) for at in range(8)])  295 us
    ppermute x84, starting transfers between devices, swap(): return lax.ppermute(value, PLANE, [(at, at ^ mask) for at in range(8)])  59.7 us
    dot_general x28, matrix products, dot_tn(): lax.dot_general(left, right, (((0,), (0,)), ((), ())), preferred_element_...  54.1 us
    unnamed x574, local copies, waits for them, and re-layouts  52.3 us
    pallas_call x2, Pallas kernels, attend_back(): pl.pallas_call(lambda *refs: attend_back_kernel(size, size ** (-0.5), *re...  38.2 us
    ppermute x18, starting transfers between devices, swap_dp(): return lax.ppermute(value, 'dp', [(at, at ^ mask) for at in range(count)])  36.4 us
    dot_general x12, matrix products, dot(): return jnp.dot(left, right, preferred_element_type=FULL)  25.1 us
    pallas_call x2, Pallas kernels, attend(): pl.pallas_call(lambda *refs: attend_kernel(size, size ** (-0.5), *refs),...  24.4 us
  transfers between devices with their start and end apart: 106, of which 44 were waited for; matrix products, arithmetic and copies ran while one was open for 35% of the time, Pallas kernels for 3%

profile of v3, /device:TPU:0, one launch (start us, length us, event | category | flops | bytes accessed | tf_op | source)
XLA Modules:
  0.0 882.4 jit_solution(9453839849546192659)
XLA Ops:
  81.5 17.7 %collective-permute-done.12 = bf16[768,768]{1,0:T(8,128)(2,1)} collective-permute-done((bf16[768,768]{1,0:T(8,128)(2,1)}, bf16[768,768]{1,0:T(8,128)(2,1)}, u32[]{:S(2)}, u32[]{:S(2)}) %collective-permute-start.12) | collective-permute-done | bytes 1179680 | tf_op jit(solution)/shard_map/ppermute | solution.py:19
  133.6 17.7 %collective-permute-done.14 = bf16[384,576]{1,0:T(8,128)(2,1)} collective-permute-done((bf16[384,576]{1,0:T(8,128)(2,1)S(1)}, bf16[384,576]{1,0:T(8,128)(2,1)}, u32[]{:S(2)}, u32[]{:S(2)}) %collective-permute-start.14) | collective-permute-done | bytes 442400 | tf_op jit(solution)/shard_map/ppermute | solution.py:19
  169.0 12.4 %attention_forward.2 = (bf16[3,128,192]{2,1,0:T(8,128)(2,1)}, bf16[3,128,192]{2,1,0:T(8,128)(2,1)}, bf16[3,128,192]{2,1,0:T(8,128)(2,1)}, bf16[3,128,192]{2,1,0:T(8,128)(2,1)}, f32[3,512,3]{2,1,0:T(8,128)}) custom-call(bf16[3,128,576]{2,1,0:T(8,128)(2,1)} %maximum_select_fusion.refs_0_, bf16[3,128,576]{2,1,0:T(8,128)(2,1)} %bitcast.46.refs_1_, ...), custom_call_target="tpu_custom_call" | custom-call | flops 1207959552 | bytes 4128768 | tf_op jit(solution)/shard_map/attention_forward/pallas_call | solution.py:147
  202.5 9.1 %collective-permute-done.22 = bf16[384,192]{1,0:T(8,128)(2,1)} collective-permute-done((bf16[384,192]{1,0:T(8,128)(2,1)}, bf16[384,192]{1,0:T(8,128)(2,1)}, u32[]{:S(2)}, u32[]{:S(2)}) %collective-permute-start.22) | collective-permute-done | bytes 147488 | tf_op jit(solution)/shard_map/ppermute | solution.py:19
  226.4 10.9 %collective-permute-done.31 = bf16[768,768]{1,0:T(8,128)(2,1)S(1)} collective-permute-done((bf16[768,768]{1,0:T(8,128)(2,1)S(1)}, bf16[768,768]{1,0:T(8,128)(2,1)S(1)}, u32[]{:S(2)}, u32[]{:S(2)}) %collective-permute-start.31) | collective-permute-done | bytes 1179680 | tf_op jit(solution)/shard_map/ppermute | solution.py:19
  258.4 8.8 collective-permute-done.33
  269.1 10.9 %collective-permute-done.35 = bf16[384,576]{1,0:T(8,128)(2,1)} collective-permute-done((bf16[384,576]{1,0:T(8,128)(2,1)S(1)}, bf16[384,576]{1,0:T(8,128)(2,1)}, u32[]{:S(2)}, u32[]{:S(2)}) %collective-permute-start.35) | collective-permute-done | bytes 442400 | tf_op jit(solution)/shard_map/ppermute | solution.py:19
  293.4 12.0 %attention_forward.3 = (bf16[3,128,192]{2,1,0:T(8,128)(2,1)}, bf16[3,128,192]{2,1,0:T(8,128)(2,1)}, bf16[3,128,192]{2,1,0:T(8,128)(2,1)}, bf16[3,128,192]{2,1,0:T(8,128)(2,1)}, f32[3,512,3]{2,1,0:T(8,128)}) custom-call(bf16[3,128,576]{2,1,0:T(8,128)(2,1)} %maximum_select_fusion.1.refs_0_, bf16[3,128,576]{2,1,0:T(8,128)(2,1)} %bitcast.72.refs_1_, ...), custom_call_target="tpu_custom_call" | custom-call | flops 1207959552 | bytes 4128768 | tf_op jit(solution)/shard_map/attention_forward/pallas_call | solution.py:147
  317.7 25.8 %collective-permute-done.40 = bf16[384,192]{1,0:T(8,128)(2,1)S(1)} collective-permute-done((bf16[384,192]{1,0:T(8,128)(2,1)S(1)}, bf16[384,192]{1,0:T(8,128)(2,1)S(1)}, u32[]{:S(2)}, u32[]{:S(2)}) %collective-permute-start.40) | collective-permute-done | bytes 147488 | tf_op jit(solution)/shard_map/ppermute | solution.py:19
  386.5 19.1 %attention_backward.2 = (bf16[4,3,128,192]{3,2,1,0:T(8,128)(2,1)}, f32[4,3,128,384]{3,2,1,0:T(8,128)}, f32[4,3,128,384]{3,2,1,0:T(8,128)}) custom-call(bf16[3,128,576]{2,1,0:T(8,128)(2,1)} %maximum_select_fusion.1.refs_0_, bf16[3,128,576]{2,1,0:T(8,128)(2,1)} %bitcast.72.refs_1_, bf16[3,128,576]{2,1,0:T(8,128)(2,1)} %bitcast.73.refs_2_, ...), custom_call_target="tpu_custom_call" | custom-call | flops 3019898880 | bytes 9437184 | tf_op jit(solution)/shard_map/attention_backward/pallas_call | solution.py:217
  420.2 6.4 collective-permute-done.49
  433.6 23.1 %collective-permute-done.56 = bf16[768,768]{0,1:T(8,128)(2,1)S(1)} collective-permute-done((bf16[768,768]{0,1:T(8,128)(2,1)S(1)}, bf16[768,768]{0,1:T(8,128)(2,1)S(1)}, u32[]{:S(2)}, u32[]{:S(2)}) %collective-permute-start.56) | collective-permute-done | bytes 1179680 | tf_op jit(solution)/shard_map/ppermute | solution.py:19
  471.2 8.8 %collective-permute-done.60 = bf16[384,576]{1,0:T(8,128)(2,1)S(1)} collective-permute-done((bf16[384,576]{1,0:T(8,128)(2,1)S(1)}, bf16[384,576]{1,0:T(8,128)(2,1)S(1)}, u32[]{:S(2)}, u32[]{:S(2)}) %collective-permute-start.60) | collective-permute-done | bytes 442400 | tf_op jit(solution)/shard_map/ppermute | solution.py:19
  555.1 18.4 %collective-permute-done.69 = bf16[768,768]{0,1:T(8,128)(2,1)S(1)} collective-permute-done((bf16[768,768]{0,1:T(8,128)(2,1)S(1)}, bf16[768,768]{0,1:T(8,128)(2,1)S(1)}, u32[]{:S(2)}, u32[]{:S(2)}) %collective-permute-start.69) | collective-permute-done | bytes 1179680 | tf_op jit(solution)/shard_map/ppermute | solution.py:19
  582.1 19.1 %attention_backward.3 = (bf16[4,3,128,192]{3,2,1,0:T(8,128)(2,1)}, f32[4,3,128,384]{3,2,1,0:T(8,128)}, f32[4,3,128,384]{3,2,1,0:T(8,128)}) custom-call(bf16[3,128,576]{2,1,0:T(8,128)(2,1)} %maximum_select_fusion.refs_0_, bf16[3,128,576]{2,1,0:T(8,128)(2,1)} %bitcast.46.refs_1_, bf16[3,128,576]{2,1,0:T(8,128)(2,1)} %bitcast.47.refs_2_, ...), custom_call_target="tpu_custom_call" | custom-call | flops 3019898880 | bytes 9437184 | tf_op jit(solution)/shard_map/attention_backward/pallas_call | solution.py:217
  615.8 16.2 %collective-permute-done.71 = bf16[768,768]{0,1:T(8,128)(2,1)} collective-permute-done((bf16[768,768]{0,1:T(8,128)(2,1)}, bf16[768,768]{0,1:T(8,128)(2,1)}, u32[]{:S(2)}, u32[]{:S(2)}) %collective-permute-start.71) | collective-permute-done | bytes 1179680 | tf_op jit(solution)/shard_map/ppermute | solution.py:19
  659.9 8.9 %collective-permute-done.76 = bf16[384,576]{1,0:T(8,128)(2,1)} collective-permute-done((bf16[384,576]{1,0:T(8,128)(2,1)}, bf16[384,576]{1,0:T(8,128)(2,1)}, u32[]{:S(2)}, u32[]{:S(2)}) %collective-permute-start.76) | collective-permute-done | bytes 442400 | tf_op jit(solution)/shard_map/ppermute | solution.py:19
  699.1 12.4 %collective-permute-done.99 = bf16[768,384]{0,1:T(8,128)(2,1)S(1)} collective-permute-done((bf16[768,384]{0,1:T(8,128)(2,1)S(1)}, bf16[768,384]{0,1:T(8,128)(2,1)S(1)}, u32[]{:S(2)}, u32[]{:S(2)}) %collective-permute-start.99) | collective-permute-done | bytes 589856 | tf_op jit(solution)/shard_map/ppermute | solution.py:19
  714.1 13.5 %collective-permute-done.98 = bf16[768,384]{0,1:T(8,128)(2,1)} collective-permute-done((bf16[768,384]{0,1:T(8,128)(2,1)}, bf16[768,384]{0,1:T(8,128)(2,1)}, u32[]{:S(2)}, u32[]{:S(2)}) %collective-permute-start.98) | collective-permute-done | bytes 589856 | tf_op jit(solution)/shard_map/ppermute | solution.py:19
  751.1 8.4 reduce-scatter.9.cloned.1.call-done
  764.2 17.6 %collective-permute-done.100 = bf16[192,768]{1,0:T(8,128)(2,1)S(1)} collective-permute-done((bf16[192,768]{1,0:T(8,128)(2,1)}, bf16[192,768]{1,0:T(8,128)(2,1)S(1)}, u32[]{:S(2)}, u32[]{:S(2)}) %collective-permute-start.100) | collective-permute-done | bytes 294944 | tf_op jit(solution)/shard_map/ppermute | solution.py:19
  793.2 12.5 %collective-permute-done.83 = bf16[768,384]{1,0:T(8,128)(2,1)S(1)} collective-permute-done((bf16[768,384]{1,0:T(8,128)(2,1)S(1)}, bf16[768,384]{1,0:T(8,128)(2,1)S(1)}, u32[]{:S(2)}, u32[]{:S(2)}) %collective-permute-start.83) | collective-permute-done | bytes 589856 | tf_op jit(solution)/shard_map/ppermute | solution.py:19
  820.8 7.6 collective-permute-done.91
  856.5 7.7 collective-permute-start.88
  (1131 shorter events, 539.8 us)
Async XLA Ops:
  7.2 104.6 %all-gather.3.cloned.1.call-start = ((), (), s32[]{:S(2)}) async-start(), calls=%async_computation.2 | async-start | bytes 1474560 | tf_op jit(solution)/shard_map/all_gather | solution.py:558
  36.7 119.4 %all-gather.5.cloned.1.call-start = ((), (), s32[]{:S(2)}) async-start(), calls=%async_computation.3 | async-start | bytes 2211840 | tf_op jit(solution)/shard_map/all_gather | solution.py:562
  47.8 32.1 %collective-permute-start.5 = (f32[2,3,2304]{2,0,1:T(2,128)}, f32[2,3,2304]{2,0,1:T(2,128)}, u32[]{:S(2)}, u32[]{:S(2)}) collective-permute-start(f32[2,3,2304]{2,0,1:T(2,128)} %get-tuple-element.470), channel_id=1, source_target_pairs={{0,24},{8,16},{16,8},{24,0},{1,25},{9,17},{17,9},{25,1},{2,26},{10... | collective-permute-start | bytes 165896 | tf_op jit(solution)/shard_map/ppermute | solution.py:23
  114.8 599.0 %reduce-scatter.7.cloned.1.call-start = ((), (), s32[]{:S(2)}) async-start(), calls=%async_computation.4 | async-start | bytes 2211840 | tf_op jit(solution)/shard_map/reduce_scatter | solution.py:655
  127.7 34.3 %collective-permute-start.26 = (bf16[768,384]{1,0:T(8,128)(2,1)}, bf16[768,384]{1,0:T(8,128)(2,1)}, u32[]{:S(2)}, u32[]{:S(2)}) collective-permute-start(bf16[768,384]{1,0:T(8,128)(2,1)} %get-tuple-element.118), channel_id=1, source_target_pairs={{0,4},{1,5},{2,6},{3,7},{4,0},{5,1},{6,2},{7,3},{8,12},{9,13},{10,... | collective-permute-start | bytes 1769480 | tf_op jit(solution)/shard_map/ppermute | solution.py:19
  130.6 32.9 %collective-permute-start.17 = (bf16[384,576]{1,0:T(8,128)(2,1)}, bf16[384,576]{1,0:T(8,128)(2,1)}, u32[]{:S(2)}, u32[]{:S(2)}) collective-permute-start(bf16[384,576]{1,0:T(8,128)(2,1)} %get-tuple-element.361), channel_id=1, source_target_pairs={{0,2},{1,3},{2,0},{3,1},{4,6},{5,7},{6,4},{7,5},{8,10},{9,11},{10,... | collective-permute-start | bytes 1327112 | tf_op jit(solution)/shard_map/ppermute | solution.py:19
  162.0 51.3 %collective-permute-start.25 = (bf16[768,768]{1,0:T(8,128)(2,1)}, bf16[768,768]{1,0:T(8,128)(2,1)}, u32[]{:S(2)}, u32[]{:S(2)}) collective-permute-start(bf16[768,768]{1,0:T(8,128)(2,1)} %pad_maximum_fusion.20), channel_id=1, source_target_pairs={{0,4},{1,5},{2,6},{3,7},{4,0},{5,1},{6,2},{7,3},{8,12},{9,13},{10,... | collective-permute-start | bytes 3538952 | tf_op jit(solution)/shard_map/ppermute | solution.py:19
  163.5 36.2 %collective-permute-start.30 = (bf16[768,384]{1,0:T(8,128)(2,1)}, bf16[768,384]{1,0:T(8,128)(2,1)}, u32[]{:S(2)}, u32[]{:S(2)}) collective-permute-start(bf16[768,384]{1,0:T(8,128)(2,1)} %get-tuple-element.126), channel_id=1, source_target_pairs={{0,1},{1,0},{2,3},{3,2},{4,5},{5,4},{6,7},{7,6},{8,9},{9,8},{10,11... | collective-permute-start | bytes 1769480 | tf_op jit(solution)/shard_map/ppermute | solution.py:19
  167.5 47.8 %collective-permute-start.27 = (bf16[768,768]{1,0:T(8,128)(2,1)}, bf16[768,768]{1,0:T(8,128)(2,1)}, u32[]{:S(2)}, u32[]{:S(2)}) collective-permute-start(bf16[768,768]{1,0:T(8,128)(2,1)} %pad_maximum_fusion.21), channel_id=1, source_target_pairs={{0,1},{1,0},{2,3},{3,2},{4,5},{5,4},{6,7},{7,6},{8,9},{9,8},{10,11... | collective-permute-start | bytes 3538952 | tf_op jit(solution)/shard_map/ppermute | solution.py:19
  258.0 50.4 %collective-permute-start.43 = (bf16[768,384]{1,0:T(8,128)(2,1)S(1)}, bf16[768,384]{1,0:T(8,128)(2,1)}, u32[]{:S(2)}, u32[]{:S(2)}) collective-permute-start(bf16[768,384]{1,0:T(8,128)(2,1)S(1)} %get-tuple-element.137), channel_id=1, source_target_pairs={{0,1},{1,0},{2,3},{3,2},{4,5},{5,4},{6,7},{7,6},{8,9},{9,8},{10,11... | collective-permute-start | bytes 1769480 | tf_op jit(solution)/shard_map/ppermute | solution.py:19
  309.6 35.8 %collective-permute-start.44 = (bf16[768,768]{1,0:T(8,128)(2,1)S(1)}, bf16[768,768]{1,0:T(8,128)(2,1)S(1)}, u32[]{:S(2)}, u32[]{:S(2)}) collective-permute-start(bf16[768,768]{1,0:T(8,128)(2,1)S(1)} %pad_maximum_fusion.23), channel_id=1, source_target_pairs={{0,4},{1,5},{2,6},{3,7},{4,0},{5,1},{6,2},{7,3},{8,12},{9,13},{10,... | collective-permute-start | bytes 3538952 | tf_op jit(solution)/shard_map/ppermute | solution.py:19
  310.3 36.4 %collective-permute-start.46 = (bf16[768,768]{1,0:T(8,128)(2,1)S(1)}, bf16[768,768]{1,0:T(8,128)(2,1)S(1)}, u32[]{:S(2)}, u32[]{:S(2)}) collective-permute-start(bf16[768,768]{1,0:T(8,128)(2,1)S(1)} %pad_maximum_fusion.24), channel_id=1, source_target_pairs={{0,1},{1,0},{2,3},{3,2},{4,5},{5,4},{6,7},{7,6},{8,9},{9,8},{10,11... | collective-permute-start | bytes 3538952 | tf_op jit(solution)/shard_map/ppermute | solution.py:19
  311.0 32.5 %collective-permute-start.40 = (bf16[384,192]{1,0:T(8,128)(2,1)S(1)}, bf16[384,192]{1,0:T(8,128)(2,1)S(1)}, u32[]{:S(2)}, u32[]{:S(2)}) collective-permute-start(bf16[384,192]{1,0:T(8,128)(2,1)S(1)} %bitcast.675), channel_id=1, source_target_pairs={{0,4},{1,5},{2,6},{3,7},{4,0},{5,1},{6,2},{7,3},{8,12},{9,13},{10,... | collective-permute-start | bytes 442376 | tf_op jit(solution)/shard_map/ppermute | solution.py:19
  518.4 33.6 %collective-permute-start.67 = (bf16[768,1536]{0,1:T(8,128)(2,1)}, bf16[768,1536]{0,1:T(8,128)(2,1)}, u32[]{:S(2)}, u32[]{:S(2)}) collective-permute-start(bf16[768,1536]{0,1:T(8,128)(2,1)} %convolution_convert_fusion), channel_id=1, source_target_pairs={{0,2},{1,3},{2,0},{3,1},{4,6},{5,7},{6,4},{7,5},{8,10},{9,11},{10,... | collective-permute-start | bytes 7077896 | tf_op jit(solution)/shard_map/ppermute | solution.py:19
  540.9 35.5 %collective-permute-start.63 = (bf16[384,192]{1,0:T(8,128)(2,1)S(1)}, bf16[384,192]{1,0:T(8,128)(2,1)S(1)}, u32[]{:S(2)}, u32[]{:S(2)}) collective-permute-start(bf16[384,192]{1,0:T(8,128)(2,1)S(1)} %get-tuple-element.450), channel_id=1, source_target_pairs={{0,1},{1,0},{2,3},{3,2},{4,5},{5,4},{6,7},{7,6},{8,9},{9,8},{10,11... | collective-permute-start | bytes 442376 | tf_op jit(solution)/shard_map/ppermute | solution.py:19
  545.5 32.3 %collective-permute-start.64 = (bf16[384,192]{1,0:T(8,128)(2,1)S(1)}, bf16[384,192]{1,0:T(8,128)(2,1)S(1)}, u32[]{:S(2)}, u32[]{:S(2)}) collective-permute-start(bf16[384,192]{1,0:T(8,128)(2,1)S(1)} %get-tuple-element.451), channel_id=1, source_target_pairs={{0,4},{1,5},{2,6},{3,7},{4,0},{5,1},{6,2},{7,3},{8,12},{9,13},{10,... | collective-permute-start | bytes 442376 | tf_op jit(solution)/shard_map/ppermute | solution.py:19
  547.5 33.9 %collective-permute-start.65 = (bf16[384,192]{1,0:T(8,128)(2,1)S(1)}, bf16[384,192]{1,0:T(8,128)(2,1)S(1)}, u32[]{:S(2)}, u32[]{:S(2)}) collective-permute-start(bf16[384,192]{1,0:T(8,128)(2,1)S(1)} %get-tuple-element.449), channel_id=1, source_target_pairs={{0,5},{1,4},{2,7},{3,6},{4,1},{5,0},{6,3},{7,2},{8,13},{9,12},{10,... | collective-permute-start | bytes 442376 | tf_op jit(solution)/shard_map/ppermute | solution.py:19
  601.2 36.4 %collective-permute-start.70 = (f32[4,3,128,384]{3,2,1,0:T(8,128)}, f32[4,3,128,384]{3,2,1,0:T(8,128)}, u32[]{:S(2)}, u32[]{:S(2)}) collective-permute-start(f32[4,3,128,384]{3,2,1,0:T(8,128)} %get-tuple-element.174), channel_id=1, source_target_pairs={{0,2},{1,3},{2,0},{3,1},{4,6},{5,7},{6,4},{7,5},{8,10},{9,11},{10,... | collective-permute-start | bytes 7077896 | tf_op jit(solution)/shard_map/ppermute | solution.py:19
  654.6 104.9 %reduce-scatter.9.cloned.1.call-start = ((), (), s32[]{:S(2)}) async-start(), calls=%async_computation.5 | async-start | bytes 1474560 | tf_op jit(solution)/shard_map/reduce_scatter | solution.py:655
  688.6 51.0 %collective-permute-start.77 = (f32[3,128,768]{2,1,0:T(8,128)}, f32[3,128,768]{2,1,0:T(8,128)}, u32[]{:S(2)}, u32[]{:S(2)}) collective-permute-start(f32[3,128,768]{2,1,0:T(8,128)} %get-tuple-element.330), channel_id=1, source_target_pairs={{0,1},{1,0},{2,3},{3,2},{4,5},{5,4},{6,7},{7,6},{8,9},{9,8},{10,11... | collective-permute-start | bytes 3538952 | tf_op jit(solution)/shard_map/ppermute | solution.py:19
  695.8 47.4 %collective-permute-start.78 = (bf16[768,1536]{1,0:T(8,128)(2,1)}, bf16[768,1536]{1,0:T(8,128)(2,1)}, u32[]{:S(2)}, u32[]{:S(2)}) collective-permute-start(bf16[768,1536]{1,0:T(8,128)(2,1)} %pad_maximum_fusion.12), channel_id=1, source_target_pairs={{0,2},{1,3},{2,0},{3,1},{4,6},{5,7},{6,4},{7,5},{8,10},{9,11},{10,... | collective-permute-start | bytes 7077896 | tf_op jit(solution)/shard_map/ppermute | solution.py:19
  696.0 31.6 %collective-permute-start.98 = (bf16[768,384]{0,1:T(8,128)(2,1)}, bf16[768,384]{0,1:T(8,128)(2,1)}, u32[]{:S(2)}, u32[]{:S(2)}) collective-permute-start(bf16[768,384]{0,1:T(8,128)(2,1)} %add_convert_fusion.12), channel_id=1, source_target_pairs={{0,1},{1,0},{2,3},{3,2},{4,5},{5,4},{6,7},{7,6},{8,9},{9,8},{10,11... | collective-permute-start | bytes 1769480 | tf_op jit(solution)/shard_map/ppermute | solution.py:19
  746.5 42.3 %collective-permute-start.82 = (bf16[768,768]{1,0:T(8,128)(2,1)}, bf16[768,768]{1,0:T(8,128)(2,1)}, u32[]{:S(2)}, u32[]{:S(2)}) collective-permute-start(bf16[768,768]{1,0:T(8,128)(2,1)} %add_convert_fusion), channel_id=1, source_target_pairs={{0,4},{1,5},{2,6},{3,7},{4,0},{5,1},{6,2},{7,3},{8,12},{9,13},{10,... | collective-permute-start | bytes 3538952 | tf_op jit(solution)/shard_map/ppermute | solution.py:19
  833.7 38.6 %collective-permute-start.95 = (bf16[2,192,384]{2,1,0:T(8,128)(2,1)S(1)}, bf16[2,192,384]{2,1,0:T(8,128)(2,1)}, u32[]{:S(2)}, u32[]{:S(2)}) collective-permute-start(bf16[2,192,384]{2,1,0:T(8,128)(2,1)S(1)} %pad_maximum_fusion.57), channel_id=1, source_target_pairs={{0,2},{1,3},{2,0},{3,1},{4,6},{5,7},{6,4},{7,5},{8,10},{9,11},{10,... | collective-permute-start | bytes 884744 | tf_op jit(solution)/shard_map/ppermute | solution.py:19
  (349 other events, 3093.3 us)
Sparse Core Ops, SparseCore 0:
  36.8 38.3 all-gather.2
  114.9 41.1 all-gather.4
  654.7 38.2 reduce-scatter.6
  731.1 28.3 reduce-scatter.8
